TPU v7x, 256 devices: a whole 4x4x8 slice. The times are simulated.
256 devices in a mesh: orb: 4 (over y), grid: 64 (over z, x, core).
Axes of the slice: x: 4, y: 4, z: 8, core: 2. Of those that a mesh axis runs over, the one named last changes fastest.
Arguments:
- orbitals: float32 [4, 768, 192, 256], P('orb', 'grid'), may hold values from -6 to 6
- potential: float32 [768, 192, 256], P('grid'), may hold values from -4 to 0
- trial_potential: float32 [768, 192, 256], P('grid'), may hold values from -6 to 6
- eigenvalues: float32 [4], P('orb'), may hold values from -3 to 0
- frequency: float32 [1], replicated, may hold values from 1 to 8
Outputs:
- solutions: float32 [4, 768, 192, 256], P('orb', 'grid')
- density: float32 [768, 192, 256], P('grid', 'orb')
All inputs are finite; a program needn't handle non-finite values.
Results may differ from a plain program's by a relative error of at most 0.0001.
Values sent between devices are 32-bit elements; how exact they have to be, the bound alone decides.
No kernel may reach another device: no remote copies, remote signals or barrier semaphores. Data moves between devices by JAX's collectives and lax.ppermute only.
A program may use at most 192 MiB of HBM per device.

v0:
```python
import jax
import jax.numpy as jnp
from jax import lax
from jax.sharding import PartitionSpec as P

ITERS = 2


STENCIL = (
    -5369.0 / 1800.0,
    12.0 / 7.0,
    -15.0 / 56.0,
    10.0 / 189.0,
    -1.0 / 112.0,
    2.0 / 1925.0,
    -1.0 / 16632.0,
)
SPACING = 0.75


def extended(value, sides, width):
    for axis, dim in sides:
        count, length = (lax.axis_size(axis), value.shape[dim])
        up = [(i, (i + 1) % count) for i in range(count - 1)]
        down = [(j, i) for i, j in up]
        last = lax.slice_in_dim(value, length - width, length, axis=dim)
        leading = lax.slice_in_dim(value, 0, width, axis=dim)
        before = lax.ppermute(last, axis, up)
        after = lax.ppermute(leading, axis, down)
        value = jnp.concatenate([before, value, after], axis=dim)
    return value


def from_everyone(value, axis):
    copies = jnp.broadcast_to(value, (lax.axis_size(axis), *value.shape))
    return lax.all_to_all(copies, axis, split_axis=0, concat_axis=0, tiled=True)


def over_copies(value, axis):
    everything = from_everyone(value, axis)
    return jnp.sum(everything, axis=0)


def packed_total(arrays, axis):
    flat, at, gathered = (jnp.concatenate([a.reshape(-1) for a in arrays]), 0, [])
    so_far = over_copies(flat, axis)
    for a in arrays:
        gathered.append(so_far[at : at + a.size].reshape(a.shape))
        at += a.size
    return tuple(gathered)


def split_up(value, dim, count):
    lengths = value.shape
    blocks = value.reshape(*lengths[:dim], count, lengths[dim] // count, *lengths[dim + 1 :])
    return jnp.moveaxis(blocks, dim, 0)


def summed_on_arrival(value, axis, dim):
    count = lax.axis_size(axis)
    blocks = lax.all_to_all(split_up(value, dim, count), axis, 0, 0, tiled=True)
    return jnp.sum(blocks, axis=0)


def shifted_hamiltonian(padded, potential, energy):
    axis_rows = padded.ndim - 3
    axis_cols = padded.ndim - 2
    length = padded.shape[axis_rows] - 12
    width = padded.shape[axis_cols]
    wrapped = jnp.concatenate(
        [padded[..., width - 6 :, :], padded, padded[..., :6, :]], axis=axis_cols
    )

    def take(row_off, col_off):
        part = lax.slice_in_dim(wrapped, 6 + row_off, 6 + row_off + length, axis=axis_rows)
        return lax.slice_in_dim(part, 6 + col_off, 6 + col_off + width, axis=axis_cols)

    center = take(0, 0)
    summed = 3.0 * STENCIL[0] * center
    for offset in range(1, 7):
        beside_all = take(offset, 0) + take(-offset, 0) + take(0, offset) + take(0, -offset)
        beside_all = beside_all + jnp.roll(center, offset, -1) + jnp.roll(center, -offset, -1)
        summed = summed + STENCIL[offset] * beside_all
    return -0.5 / (SPACING * SPACING) * summed + (potential - energy) * center


def cell_sum(first, second):
    return jnp.sum(first * second, axis=(1, 2, 3))


def spread(values):
    return values[:, None, None, None]


def body(orbitals, potential, trial_potential, eigenvalues, frequency):
    squared = frequency[0] * frequency[0]
    energy = spread(eigenvalues)

    def shifted(field):
        padded = extended(field, (("grid", 1),), 6)
        return shifted_hamiltonian(padded, potential, energy)

    def operator(field):
        return shifted(shifted(field)) + squared * field

    source = trial_potential * orbitals
    solution = jnp.zeros_like(source)
    residual = source

    def paired(vector, image):
        return packed_total((cell_sum(vector, vector), cell_sum(vector, image)), "grid")

    image = operator(residual)
    norm_now, product = paired(residual, image)
    step_size = norm_now / product
    direction = residual
    along = image
    for step in range(ITERS):
        solution = solution + spread(step_size) * direction
        residual = residual - spread(step_size) * along
        if step + 1 < ITERS:
            image = operator(residual)
            norm_next, product = paired(residual, image)
            ratio = norm_next / norm_now
            step_size = norm_next / (product - ratio * norm_next / step_size)
            direction = residual + spread(ratio) * direction
            along = image + spread(ratio) * along
            norm_now = norm_next
    response = -4.0 * jnp.sum(orbitals * shifted(solution), axis=0)
    density = summed_on_arrival(response, "orb", 1)
    return (solution, density)


def solution(mesh):
    in_specs = (
        P("orb", "grid", None, None),
        P("grid", None, None),
        P("grid", None, None),
        P("orb"),
        P(),
    )
    out_specs = (P("orb", "grid", None, None), P("grid", "orb", None))
    return jax.shard_map(body, mesh=mesh, in_specs=in_specs, out_specs=out_specs, check_vma=False)
```

profile of v0, /device:TPU:7, one launch (start us, length us, event | category | flops | bytes accessed | tf_op | source)
XLA Modules:
  0.0 448.9 jit_solution(16229465895528199553)
XLA Ops:
  6.1 5.1 %collective-permute-start.1 = (f32[1,6,192,256]{3,2,1,0:T(8,128)S(1)}, f32[1,6,192,256]{3,2,1,0:T(8,128)S(1)}, u32[]{:S(2)}, u32[]{:S(2)}) collective-permute-start(f32[1,6,192,256]{3,2,1,0:T(8,128)S(1)} %get-tuple-element.146), channel_id=1, source_target_pairs={{0,1},{1,2},{2,3},{3,4},{4,5},{5,6},{6,7},{7,8},{8,9},{9,10},{10,1... | collective-permute-start | bytes 3538952 | tf_op jit(solution)/shard_map/ppermute | solution.py:28
  21.9 3.0 fusion.335
  27.9 3.0 fusion.337
  35.1 3.0 fusion.339
  38.2 3.0 fusion.331
  44.2 22.9 %fusion.217 = f32[1,12,192,256]{3,2,1,0:T(8,128)S(1)} fusion(f32[1,12,192,256]{3,2,1,0:T(8,128)S(1)} %bitcast_multiply_fusion.5, f32[1,6,192,256]{3,2,1,0:T(8,128)} %copy-done.4, f32[1,6,192,256]{3,2,1,0:T(8,128)S(1)} %collective-permute-done, f32[1,24,198,256]{3,2,1,0:T(8,128)} %get-tuple-element.16, f32[1,24,198,256]{3,2,1,0:T(8,128)S(1)} %get-tuple-element.15, ...), kind=kLoop, calls=%fused_computation.337 | loop fusion | flops 41877504 | bytes 66060292 | tf_op jit(solution)/shard_map/add | solution.py:84
  102.0 6.5 %collective-permute-done.2 = f32[1,6,192,256]{3,2,1,0:T(8,128)S(1)} collective-permute-done((f32[1,6,192,256]{3,2,1,0:T(8,128)S(1)}, f32[1,6,192,256]{3,2,1,0:T(8,128)S(1)}, u32[]{:S(2)}, u32[]{:S(2)}) %collective-permute-start.2) | collective-permute-done | bytes 1179680 | tf_op jit(solution)/shard_map/ppermute | solution.py:29
  108.5 3.1 fusion.7
  111.6 24.8 %multiply_reduce_fusion.2 = (f32[]{:T(128)}, f32[]{:T(128)}, f32[1,12,192,256]{3,2,1,0:T(8,128)}) fusion(f32[1,12,192,256]{3,2,1,0:T(8,128)S(1)} %bitcast_multiply_fusion.5, f32[]{:T(128)} %bitcast.4, f32[1,12,192,256]{3,2,1,0:T(8,128)S(1)} %fusion.217, f32[12,192,256]{2,1,0:T(8,128)} %param.6, f32[]{:T(128)} %bitcast.37, ...), kind=kLoop, calls=%fused_computation.425 | loop fusion | flops 45416448 | bytes 68419600 | tf_op jit(solution)/shard_map/reduce_sum | solution.py:88
  137.7 18.8 %all_to_all.17 = f32[64,1,2]{2,1,0:T(1,128)S(1)} all-to-all(f32[64,1,2]{2,1,0:T(1,128)S(1)} %broadcast_in_dim.7), channel_id=1, replica_groups=mesh['orb'=4,'grid'=64] {'grid'}, dimensions={0} | all-to-all | bytes 1024 | tf_op jit(solution)/shard_map/all_to_all | solution.py:36
  184.3 5.1 %collective-permute-start.5 = (f32[1,6,192,256]{3,2,1,0:T(8,128)S(1)}, f32[1,6,192,256]{3,2,1,0:T(8,128)S(1)}, u32[]{:S(2)}, u32[]{:S(2)}) collective-permute-start(f32[1,6,192,256]{3,2,1,0:T(8,128)S(1)} %get-tuple-element.94), channel_id=1, source_target_pairs={{0,1},{1,2},{2,3},{3,4},{4,5},{5,6},{6,7},{7,8},{8,9},{9,10},{10,1... | collective-permute-start | bytes 3538952 | tf_op jit(solution)/shard_map/ppermute | solution.py:28
  189.4 3.0 fusion.313
  198.2 3.1 collective-permute-done.4
  202.5 4.8 %fusion.5 = (f32[1,24,198,256]{3,2,1,0:T(8,128)}, f32[1,24,198,256]{3,2,1,0:T(8,128)}) fusion(f32[1,6,192,256]{3,2,1,0:T(8,128)S(1)} %collective-permute-done.4, f32[1,12,192,256]{3,2,1,0:T(8,128)S(1)} %get-tuple-element.5, f32[1,6,192,256]{3,2,1,0:T(8,128)S(1)} %collective-permute-done.5), kind=kLoop, calls=%fused_computation.116 | loop fusion | flops 12165120 | bytes 14450688 | tf_op jit(solution)/shard_map/concatenate | solution.py:70
  207.3 28.6 %fusion.120 = f32[1,12,192,256]{3,2,1,0:T(8,128)S(1)} fusion(f32[1,12,192,256]{3,2,1,0:T(8,128)S(1)} %get-tuple-element.5, f32[1,6,192,256]{3,2,1,0:T(8,128)} %copy-done.8, f32[1,6,192,256]{3,2,1,0:T(8,128)S(1)} %collective-permute-done.4, f32[1,24,198,256]{3,2,1,0:T(8,128)} %get-tuple-element.12, f32[1,24,198,256]{3,2,1,0:T(8,128)} %get-tuple-element.11, ...), kind=kLoop, calls=%fused_computation.240 | loop fusion | flops 41877504 | bytes 66060292 | tf_op jit(solution)/shard_map/add | solution.py:84
  255.9 6.5 %collective-permute-start.7 = (f32[1,6,192,256]{3,2,1,0:T(8,128)S(1)}, f32[1,6,192,256]{3,2,1,0:T(8,128)S(1)}, u32[]{:S(2)}, u32[]{:S(2)}) collective-permute-start(f32[1,6,192,256]{3,2,1,0:T(8,128)S(1)} %get-tuple-element.63), channel_id=1, source_target_pairs={{0,1},{1,2},{2,3},{3,4},{4,5},{5,6},{6,7},{7,8},{8,9},{9,10},{10,1... | collective-permute-start | bytes 3538952 | tf_op jit(solution)/shard_map/ppermute | solution.py:28
  275.5 6.5 %collective-permute-done.6 = f32[1,6,192,256]{3,2,1,0:T(8,128)S(1)} collective-permute-done((f32[1,6,192,256]{3,2,1,0:T(8,128)S(1)}, f32[1,6,192,256]{3,2,1,0:T(8,128)S(1)}, u32[]{:S(2)}, u32[]{:S(2)}) %collective-permute-start.6) | collective-permute-done | bytes 1179680 | tf_op jit(solution)/shard_map/ppermute | solution.py:29
  282.0 4.6 %fusion.3 = (f32[1,24,198,256]{3,2,1,0:T(8,128)}, f32[1,24,198,256]{3,2,1,0:T(8,128)}) fusion(f32[1,6,192,256]{3,2,1,0:T(8,128)S(1)} %collective-permute-done.6, f32[1,12,192,256]{3,2,1,0:T(8,128)S(1)} %fusion.120, f32[1,6,192,256]{3,2,1,0:T(8,128)S(1)} %collective-permute-done.7), kind=kLoop, calls=%fused_computation.110 | loop fusion | flops 12165120 | bytes 14450688 | tf_op jit(solution)/shard_map/concatenate | solution.py:70
  286.5 33.6 %fusion.275 = f32[]{:T(128)} fusion(f32[1,12,192,256]{3,2,1,0:T(8,128)S(1)} %get-tuple-element.5, f32[1,12,192,256]{3,2,1,0:T(8,128)S(1)} %fusion.120, f32[1,12,192,6]{3,2,1,0:T(8,128)} %get-tuple-element.66, f32[1,12,192,250]{3,2,1,0:T(8,128)} %get-tuple-element.68, f32[1,12,192,250]{3,2,1,0:T(8,128)} %get-tuple-element.67, ...), kind=kLoop, calls=%fused_computation.426 | loop fusion | flops 44236800 | bytes 66060300 | tf_op jit(solution)/shard_map/reduce_sum | solution.py:88
  321.5 15.9 %all_to_all.18 = f32[64,1,2]{2,1,0:T(1,128)S(1)} all-to-all(f32[64,1,2]{2,1,0:T(1,128)S(1)} %broadcast_in_dim.8), channel_id=1, replica_groups=mesh['orb'=4,'grid'=64] {'grid'}, dimensions={0} | all-to-all | bytes 1024 | tf_op jit(solution)/shard_map/all_to_all | solution.py:36
  356.0 3.0 fusion.285
  367.4 5.3 %collective-permute-start.9 = (f32[1,6,192,256]{3,2,1,0:T(8,128)S(1)}, f32[1,6,192,256]{3,2,1,0:T(8,128)S(1)}, u32[]{:S(2)}, u32[]{:S(2)}) collective-permute-start(f32[1,6,192,256]{3,2,1,0:T(8,128)S(1)} %get-tuple-element.42), channel_id=1, source_target_pairs={{0,1},{1,2},{2,3},{3,4},{4,5},{5,6},{6,7},{7,8},{8,9},{9,10},{10,1... | collective-permute-start | bytes 3538952 | tf_op jit(solution)/shard_map/ppermute | solution.py:28
  388.5 23.9 %fusion.22 = f32[1,12,192,256]{3,2,1,0:T(8,128)} fusion(f32[1,12,192,256]{3,2,1,0:T(8,128)} %param.5, f32[1,12,192,256]{3,2,1,0:T(8,128)S(1)} %multiply_add_fusion, f32[1,6,192,256]{3,2,1,0:T(8,128)} %copy-done.7, f32[1,6,192,256]{3,2,1,0:T(8,128)S(1)} %collective-permute-done.8, f32[1,24,198,256]{3,2,1,0:T(8,128)} %get-tuple-element.8, ...), kind=kLoop, calls=%fused_computation.142 | loop fusion | flops 43057152 | bytes 68419584 | tf_op jit(solution)/shard_map/mul | solution.py:129
  414.2 33.5 %all_to_all.19 = f32[4,12,48,256]{3,2,1,0:T(8,128)S(1)} all-to-all(f32[4,12,48,256]{3,2,1,0:T(8,128)S(1)} %copy.11), channel_id=1, replica_groups=mesh['orb'=4,'grid'=64] {'orb'}, dimensions={0} | all-to-all | bytes 4718592 | tf_op jit(solution)/shard_map/all_to_all | solution.py:61
  (105 shorter events, 170.1 us)
Async XLA Ops:
  3.5 37.7 %collective-permute-start = (f32[1,6,192,256]{3,2,1,0:T(8,128)S(1)}, f32[1,6,192,256]{3,2,1,0:T(8,128)S(1)}, u32[]{:S(2)}, u32[]{:S(2)}) collective-permute-start(f32[1,6,192,256]{3,2,1,0:T(8,128)S(1)} %get-tuple-element.145), channel_id=1, source_target_pairs={{1,0},{2,1},{3,2},{4,3},{5,4},{6,5},{7,6},{8,7},{9,8},{10,9},{11,1... | collective-permute-start | bytes 3538952 | tf_op jit(solution)/shard_map/ppermute | solution.py:29
  6.1 35.1 %collective-permute-start.1 = (f32[1,6,192,256]{3,2,1,0:T(8,128)S(1)}, f32[1,6,192,256]{3,2,1,0:T(8,128)S(1)}, u32[]{:S(2)}, u32[]{:S(2)}) collective-permute-start(f32[1,6,192,256]{3,2,1,0:T(8,128)S(1)} %get-tuple-element.146), channel_id=1, source_target_pairs={{0,1},{1,2},{2,3},{3,4},{4,5},{5,6},{6,7},{7,8},{8,9},{9,10},{10,1... | collective-permute-start | bytes 3538952 | tf_op jit(solution)/shard_map/ppermute | solution.py:28
  41.2 3.0 copy-start.4
  86.9 15.0 %collective-permute-start.3 = (f32[1,6,192,256]{3,2,1,0:T(8,128)S(1)}, f32[1,6,192,256]{3,2,1,0:T(8,128)S(1)}, u32[]{:S(2)}, u32[]{:S(2)}) collective-permute-start(f32[1,6,192,256]{3,2,1,0:T(8,128)S(1)} %get-tuple-element.115), channel_id=1, source_target_pairs={{0,1},{1,2},{2,3},{3,4},{4,5},{5,6},{6,7},{7,8},{8,9},{9,10},{10,1... | collective-permute-start | bytes 3538952 | tf_op jit(solution)/shard_map/ppermute | solution.py:28
  88.9 19.6 %collective-permute-start.2 = (f32[1,6,192,256]{3,2,1,0:T(8,128)S(1)}, f32[1,6,192,256]{3,2,1,0:T(8,128)S(1)}, u32[]{:S(2)}, u32[]{:S(2)}) collective-permute-start(f32[1,6,192,256]{3,2,1,0:T(8,128)S(1)} %get-tuple-element.116), channel_id=1, source_target_pairs={{1,0},{2,1},{3,2},{4,3},{5,4},{6,5},{7,6},{8,7},{9,8},{10,9},{11,1... | collective-permute-start | bytes 3538952 | tf_op jit(solution)/shard_map/ppermute | solution.py:29
  108.5 3.1 copy-start.5
  161.6 124.9 %copy-start = (f32[1,12,192,256]{3,2,1,0:T(8,128)}, f32[1,12,192,256]{3,2,1,0:T(8,128)S(1)}, u32[]{:S(2)}) copy-start(f32[1,12,192,256]{3,2,1,0:T(8,128)S(1)} %get-tuple-element.5) | copy-start | bytes 7077892
  181.7 19.6 %collective-permute-start.4 = (f32[1,6,192,256]{3,2,1,0:T(8,128)S(1)}, f32[1,6,192,256]{3,2,1,0:T(8,128)S(1)}, u32[]{:S(2)}, u32[]{:S(2)}) collective-permute-start(f32[1,6,192,256]{3,2,1,0:T(8,128)S(1)} %get-tuple-element.93), channel_id=1, source_target_pairs={{1,0},{2,1},{3,2},{4,3},{5,4},{6,5},{7,6},{8,7},{9,8},{10,9},{11,1... | collective-permute-start | bytes 3538952 | tf_op jit(solution)/shard_map/ppermute | solution.py:29
  184.3 18.2 %collective-permute-start.5 = (f32[1,6,192,256]{3,2,1,0:T(8,128)S(1)}, f32[1,6,192,256]{3,2,1,0:T(8,128)S(1)}, u32[]{:S(2)}, u32[]{:S(2)}) collective-permute-start(f32[1,6,192,256]{3,2,1,0:T(8,128)S(1)} %get-tuple-element.94), channel_id=1, source_target_pairs={{0,1},{1,2},{2,3},{3,4},{4,5},{5,6},{6,7},{7,8},{8,9},{9,10},{10,1... | collective-permute-start | bytes 3538952 | tf_op jit(solution)/shard_map/ppermute | solution.py:28
  198.2 9.0 %copy-start.2 = (f32[12,192,256]{2,1,0:T(8,128)S(1)}, f32[12,192,256]{2,1,0:T(8,128)}, u32[]{:S(2)}) copy-start(f32[12,192,256]{2,1,0:T(8,128)} %param.6) | copy-start | bytes 7077892
  202.5 4.8 %copy-start.8 = (f32[1,6,192,256]{3,2,1,0:T(8,128)}, f32[1,6,192,256]{3,2,1,0:T(8,128)S(1)}, u32[]{:S(2)}) copy-start(f32[1,6,192,256]{3,2,1,0:T(8,128)S(1)} %collective-permute-done.5) | copy-start | bytes 3538948
  255.9 19.6 %collective-permute-start.7 = (f32[1,6,192,256]{3,2,1,0:T(8,128)S(1)}, f32[1,6,192,256]{3,2,1,0:T(8,128)S(1)}, u32[]{:S(2)}, u32[]{:S(2)}) collective-permute-start(f32[1,6,192,256]{3,2,1,0:T(8,128)S(1)} %get-tuple-element.63), channel_id=1, source_target_pairs={{0,1},{1,2},{2,3},{3,4},{4,5},{5,6},{6,7},{7,8},{8,9},{9,10},{10,1... | collective-permute-start | bytes 3538952 | tf_op jit(solution)/shard_map/ppermute | solution.py:28
  262.3 19.6 %collective-permute-start.6 = (f32[1,6,192,256]{3,2,1,0:T(8,128)S(1)}, f32[1,6,192,256]{3,2,1,0:T(8,128)S(1)}, u32[]{:S(2)}, u32[]{:S(2)}) collective-permute-start(f32[1,6,192,256]{3,2,1,0:T(8,128)S(1)} %get-tuple-element.64), channel_id=1, source_target_pairs={{1,0},{2,1},{3,2},{4,3},{5,4},{6,5},{7,6},{8,7},{9,8},{10,9},{11,1... | collective-permute-start | bytes 3538952 | tf_op jit(solution)/shard_map/ppermute | solution.py:29
  282.0 4.6 %copy-start.6 = (f32[1,6,192,256]{3,2,1,0:T(8,128)}, f32[1,6,192,256]{3,2,1,0:T(8,128)S(1)}, u32[]{:S(2)}) copy-start(f32[1,6,192,256]{3,2,1,0:T(8,128)S(1)} %collective-permute-done.6) | copy-start | bytes 3538948
  344.7 43.8 %copy-start.1 = (f32[1,12,192,256]{3,2,1,0:T(8,128)}, f32[1,12,192,256]{3,2,1,0:T(8,128)S(1)}, u32[]{:S(2)}) copy-start(f32[1,12,192,256]{3,2,1,0:T(8,128)S(1)} %multiply_add_fusion) | copy-start | bytes 7077892
  364.8 19.6 %collective-permute-start.8 = (f32[1,6,192,256]{3,2,1,0:T(8,128)S(1)}, f32[1,6,192,256]{3,2,1,0:T(8,128)S(1)}, u32[]{:S(2)}, u32[]{:S(2)}) collective-permute-start(f32[1,6,192,256]{3,2,1,0:T(8,128)S(1)} %get-tuple-element.41), channel_id=1, source_target_pairs={{1,0},{2,1},{3,2},{4,3},{5,4},{6,5},{7,6},{8,7},{9,8},{10,9},{11,1... | collective-permute-start | bytes 3538952 | tf_op jit(solution)/shard_map/ppermute | solution.py:29
  367.4 18.2 %collective-permute-start.9 = (f32[1,6,192,256]{3,2,1,0:T(8,128)S(1)}, f32[1,6,192,256]{3,2,1,0:T(8,128)S(1)}, u32[]{:S(2)}, u32[]{:S(2)}) collective-permute-start(f32[1,6,192,256]{3,2,1,0:T(8,128)S(1)} %get-tuple-element.42), channel_id=1, source_target_pairs={{0,1},{1,2},{2,3},{3,4},{4,5},{5,6},{6,7},{7,8},{8,9},{9,10},{10,1... | collective-permute-start | bytes 3538952 | tf_op jit(solution)/shard_map/ppermute | solution.py:28
  381.5 7.0 %copy-start.3 = (f32[12,192,256]{2,1,0:T(8,128)S(1)}, f32[12,192,256]{2,1,0:T(8,128)}, u32[]{:S(2)}) copy-start(f32[12,192,256]{2,1,0:T(8,128)} %param.6) | copy-start | bytes 7077892
  385.6 2.9 copy-start.7
where the time goes:
time: 455 us; the launch traced here: 449 us
  other arithmetic  164 us (36%)
  local copies, waits for them, and re-layouts  147 us (32%)
  blocking collectives  68.2 us (15%)
  starting transfers between devices  35.9 us (8%)
  waiting for transfers between devices  25.5 us (6%)
  between operations  8.26 us (2%)
    slice x36, local copies, waits for them, and re-layouts, shifted_hamiltonian(): jnp.roll(center, -offset, -1)  86.2 us
    reduce_sum x3, other arithmetic, cell_sum(): return jnp.sum(first * second, axis=(1, 2, 3))  61.3 us
    slice x24, local copies, waits for them, and re-layouts, shifted_hamiltonian(): jnp.roll(center, offset, -1)  57.2 us
    add x2, other arithmetic, shifted_hamiltonian(): return -0.5 / (SPACING * SPACING) * summed + (potential - energy) * center  51.4 us
    all_to_all x2, blocking collectives, from_everyone(): return lax.all_to_all(copies, axis, split_axis=0, concat_axis=0, tiled=True)  34.8 us
    all_to_all x1, blocking collectives, summed_on_arrival(): blocks = lax.all_to_all(split_up(value, dim, count), axis, 0, 0, tiled=True)  33.5 us
    mul x1, other arithmetic, body(): response = -4.0 * jnp.sum(orbitals * shifted(solution), axis=0)  23.9 us
    ppermute x5, starting transfers between devices, extended(): before = lax.ppermute(last, axis, up)  23.9 us
  transfers between devices with their start and end apart: 10, of which 8 were waited for; matrix products, arithmetic and copies ran while one was open for 14% of the time, Pallas kernels for 0%

commit v1 on v0

v1 whole, which is shorter than its diff:
```python
import functools

import jax
import jax.numpy as jnp
import ml_dtypes
import numpy as np
from jax import lax
from jax.experimental import pallas as pl
from jax.experimental.pallas import tpu as pltpu
from jax.sharding import PartitionSpec as P

STENCIL = (
    -5369.0 / 1800.0,
    12.0 / 7.0,
    -15.0 / 56.0,
    10.0 / 189.0,
    -1.0 / 112.0,
    2.0 / 1925.0,
    -1.0 / 16632.0,
)
SPACING = 0.75
COEF = tuple(-0.5 / (SPACING * SPACING) * c for c in STENCIL)
W = 6
F32, BF16 = jnp.float32, jnp.bfloat16
VM = pl.BlockSpec(memory_space=pltpu.VMEM)
SM = pl.BlockSpec(memory_space=pltpu.SMEM)
ANY = pl.BlockSpec(memory_space=pl.ANY)
MIB = 1 << 20


def in_hbm_type(array):
    return pltpu.HBM(array.shape, array.dtype)


def in_vmem(value):
    return pltpu.with_memory_space_constraint(value, pltpu.VMEM)


def in_hbm(value):
    return pltpu.with_memory_space_constraint(value, pltpu.HBM)


def circulant(n):
    m = np.zeros((n, n), np.float64)
    for k in range(1, W + 1):
        for i in range(n):
            m[i, (i + k) % n] += COEF[k]
            m[i, (i - k) % n] += COEF[k]
    high = m.astype(ml_dtypes.bfloat16)
    low = (m - high.astype(np.float64)).astype(ml_dtypes.bfloat16)
    return high, low


def plane_of(m, core):
    return m + core * (2 * W - 1 - 2 * m)


def core_index():
    return lax.rem(lax.axis_index("grid"), 2)


def rows_of(t):
    return pl.ds(pl.multiple_of(t * 8, 8), 8)


def call(kernel, out_shape, in_specs, out_specs, scratch=(), limit=24):
    return pl.pallas_call(
        kernel,
        out_shape=out_shape,
        in_specs=in_specs,
        out_specs=out_specs,
        scratch_shapes=list(scratch),
        compiler_params=pltpu.CompilerParams(vmem_limit_bytes=limit * MIB),
    )


def source_kernel(orb, trial, core_ref, ro, ri, a, b, sems):
    core = core_ref[0]

    def copies(m):
        p = plane_of(m, core)
        return (
            pltpu.make_async_copy(orb.at[0, p], a.at[m], sems.at[0, m]),
            pltpu.make_async_copy(trial.at[p], b.at[m], sems.at[1, m]),
        )

    for m in range(2 * W):
        for c in copies(m):
            c.start()
    for m in range(2 * W):
        for c in copies(m):
            c.wait()
        out = ro if m < W else ri
        out[m % W] = a[m] * b[m]


def part_rows(d, me, count, part):
    quarter = lax.rem(me + d, count)
    return quarter * part


def local_kernel(fo, fi, hi_halo, pot, orb, energy, core_ref, me_ref, mz, my, *refs, stage, count):
    gi, po, tile, own_out, kept, *parts = refs[-count - 9 : -5]
    orb_v, own, yz, sems, more_sems = refs[-5:]
    parts = [own, *parts]
    core, me = core_ref[0], me_ref[0]
    nz = fo.shape[2]
    part = own.shape[1]
    first = 0 if stage == 1 else W
    loads = [pltpu.make_async_copy(orb.at[0, plane_of(first + m, core)], orb_v.at[m], sems.at[m]) for m in range(W)]
    stores = (
        pltpu.make_async_copy(fo, kept.at[pl.ds(0, W)], more_sems.at[0]),
        pltpu.make_async_copy(fi, kept.at[pl.ds(W, W)], more_sems.at[1]),
    )
    store_own = pltpu.make_async_copy(own, own_out, more_sems.at[2])
    for c in loads:
        c.start()

    for half, ref in enumerate((fo, fi)):

        def one(m, _, ref=ref, half=half):
            v = ref[m]
            high = v.astype(BF16)
            low = (v - high.astype(F32)).astype(BF16)
            dot = functools.partial(jnp.dot, preferred_element_type=F32)
            acc = dot(high, mz[0]) + dot(low, mz[0]) + dot(high, mz[1])
            acc = acc + (dot(my[0], high) + dot(my[1], high) + dot(my[0], low))
            yz[half * W + m] = acc
            return 0

        lax.fori_loop(0, W, one, 0)

    for c in loads:
        c.wait()
    for c in stores:
        c.start()
    diag = 3.0 * COEF[0] - energy[0]
    acc = jnp.zeros((8, 128), F32)
    for d in range(count):
        start = part_rows(d, me, count, part)

        def column(t, acc, d=d, start=start):
            rows = pl.ds(pl.multiple_of(start + t * 8, 8), 8)
            for h in range(nz // 128):
                lanes = slice(128 * h, 128 * h + 128)
                line = [fo[m, rows, lanes] for m in range(W)]
                line += [fi[m, rows, lanes] for m in range(W)]
                line += [hi_halo[W - 1 - m, rows, lanes] for m in range(W)]
                for m in range(2 * W):
                    if stage < 2:
                        acc = acc + line[m] * line[m]
                    out = (pot[plane_of(m, core), rows, lanes] + diag) * line[m]
                    out = out + yz[m, rows, lanes]
                    for k in range(1, W + 1):
                        pair = line[m + k] if m < k else line[m + k] + line[m - k]
                        out = out + COEF[k] * pair
                    if m < W:
                        po[m, rows, lanes] = out
                        if stage == 1:
                            parts[d][m, rows_of(t), lanes] = orb_v[m, rows, lanes] * line[m]
                    else:
                        gi[m - W, rows, lanes] = out
                        if stage != 1:
                            at = m if stage == 2 and d else m - W
                            parts[d][at, rows_of(t), lanes] = orb_v[m - W, rows, lanes] * out
            return acc

        acc = lax.fori_loop(0, part // 8, column, acc)
    tile[...] = acc
    store_own.start()
    for c in stores:
        c.wait()
    store_own.wait()


def with_halo(po, ho, rows, lanes):
    halo = [ho[j, rows, lanes] for j in range(W)]
    outs = []
    for m in range(W):
        out = po[m, rows, lanes]
        for k in range(m + 1, W + 1):
            out = out + COEF[k] * halo[k - m - 1]
        outs.append(out)
    return outs


def halo_kernel(po, ho, *refs):
    go = refs[-1]

    def column(t, _):
        rows = rows_of(t)
        for h in range(po.shape[2] // 128):
            lanes = slice(128 * h, 128 * h + 128)
            for m, out in enumerate(with_halo(po, ho, rows, lanes)):
                go[m, rows, lanes] = out
        return 0

    lax.fori_loop(0, po.shape[1] // 8, column, 0)


def whole_sum(tile):
    return jnp.sum(tile, keepdims=True)


def broad(scalar, shape=(8, 128)):
    return jnp.broadcast_to(scalar, shape)


def sums_kernel(r, t_kept, orb, uo, ui, vi, rr_tile, tt_tile, core_ref, *refs):
    rows_out, inner, to, orb_o, r_v, ti, sems = refs[-7:]
    core = core_ref[0]
    ro, ri = r_v.at[pl.ds(0, W)], r_v.at[pl.ds(W, W)]
    loads = (
        pltpu.make_async_copy(r, r_v, sems.at[0]),
        pltpu.make_async_copy(t_kept.at[pl.ds(W, W)], ti, sems.at[1]),
        pltpu.make_async_copy(t_kept.at[pl.ds(0, W)], to, sems.at[2]),
        *(pltpu.make_async_copy(orb.at[0, plane_of(m, core)], orb_o.at[m], sems.at[3 + m]) for m in range(W)),
    )
    for c in loads:
        c.start()
    loads[0].wait()
    steps = uo.shape[1] // 8
    zero = jnp.zeros((8, 128), F32)

    def cells(t):
        for h in range(uo.shape[2] // 128):
            for m in range(W):
                yield m, rows_of(t), slice(128 * h, 128 * h + 128)

    def cross(t, acc):
        for at in cells(t):
            acc = acc + ro[at] * uo[at] + ri[at] * ui[at]
        return acc

    rr = whole_sum(rr_tile[...])
    ru = whole_sum(lax.fori_loop(0, steps, cross, zero))
    theta = broad(jnp.where(rr > 0.0, ru / jnp.where(rr > 0.0, rr, 1.0), 0.0))

    def squares(t, accs):
        s0, s1, t0, t1 = accs
        for at in cells(t):
            for r, u in ((ro, uo), (ri, ui)):
                x = u[at] - theta * r[at]
                s0, s1 = s0 + x * x, s1 + x * r[at]
            x = vi[at] - theta * ti[at]
            t0, t1 = t0 + x * x, t1 + x * ti[at]
        return s0, s1, t0, t1

    loads[1].wait()
    s0, s1, t0, t1 = lax.fori_loop(0, steps, squares, (zero,) * 4)
    row = [rr, whole_sum(tt_tile[...]), whole_sum(s0), whole_sum(s1)]
    rows_out[...] = jnp.concatenate([broad(x, (1, 128)) for x in row] + [theta[:4]], axis=0)
    inner[0], inner[1] = t0, t1
    for c in loads[2:]:
        c.wait()


def last_kernel(po, ho, to, orb, rows_in, inner, me_ref, *refs, count):
    tile, own_out, *outs, own, sem = refs[-count - 3 :]
    for done, out in zip(refs[: count - 1], outs):
        for m in range(W, 2 * W):
            out[m] = done[m]
    outs = [own, *outs]
    me = me_ref[0]
    theta = broad(rows_in[4:5])
    part = outs[0].shape[1]
    accs = inner[0], inner[1]
    for d in range(count):
        start = part_rows(d, me, count, part)

        def column(step, accs, d=d, start=start):
            t0, t1 = accs
            there = pl.ds(pl.multiple_of(start + step * 8, 8), 8)
            for h in range(po.shape[2] // 128):
                lanes = slice(128 * h, 128 * h + 128)
                for m, v in enumerate(with_halo(po, ho, there, lanes)):
                    t = to[m, there, lanes]
                    x = v - theta * t
                    t0, t1 = t0 + x * x, t1 + x * t
                    outs[d][m, rows_of(step), lanes] = orb[m, there, lanes] * v
            return t0, t1

        accs = lax.fori_loop(0, part // 8, column, accs)
        if d == 0:
            store_own = pltpu.make_async_copy(own, own_out, sem.at[0])
            store_own.start()
    lane = lax.broadcasted_iota(jnp.int32, (8, 128), 1)
    row = jnp.zeros((8, 128), F32)
    for i in range(5):
        row = jnp.where(lane == i, broad(rows_in[i : i + 1]), row)
    for i, x in enumerate(accs):
        row = jnp.where(lane == 5 + i, broad(whole_sum(x)), row)
    for i in range(tile.shape[0]):
        tile[i] = row
    store_own.wait()


def coefficient_kernel(shares, freq, out):
    w2 = freq[0] * freq[0]
    share = shares[:, 0, :]
    rr, tt, s0, s1, own, t0, t1 = (share[:, i : i + 1] for i in range(7))

    def total(x):
        return jnp.sum(x, axis=0, keepdims=True)

    rr0, tt0 = total(rr), total(tt)
    theta = tt0 / rr0
    off = jnp.broadcast_to(theta, own.shape) - own
    alpha = 1.0 / (theta + w2)
    rr1 = alpha * alpha * total(s0 - 2.0 * off * s1 + off * off * rr)
    tt1 = alpha * alpha * total(t0 - 2.0 * off * t1 + off * off * tt)
    ratio = rr1 / rr0
    beta = rr1 / (tt1 + w2 * rr1 - ratio * rr1 / alpha)
    p = alpha + beta * ratio + beta * alpha * theta
    q = -beta * alpha
    both = jnp.concatenate([broad(p, (4, 128)), broad(q, (4, 128))], axis=0)
    for i in range(out.shape[0]):
        out[i] = both


def both_of(coefs, n, shape):
    one = coefs[n]
    return tuple(broad(one[4 * i : 4 * i + 1, 0:1], shape) for i in range(2))


def solution_kernel(r, u, coefs, core_ref, sol, rbuf, ubuf, xbuf, in_sems, out_sems):
    core = core_ref[0]

    def fields(m):
        return (
            pltpu.make_async_copy(r.at[m], rbuf.at[m], in_sems.at[0, m]),
            pltpu.make_async_copy(u.at[m], ubuf.at[m], in_sems.at[1, m]),
        )

    def store(m):
        return pltpu.make_async_copy(xbuf.at[m], sol.at[0, plane_of(m, core)], out_sems.at[m])

    for m in range(2 * W):
        for c in fields(m):
            c.start()
    p, q = both_of(coefs, 0, (8, rbuf.shape[2]))
    for m in range(2 * W):
        for c in fields(m):
            c.wait()

        def row(t, _, m=m):
            rows = rows_of(t)
            xbuf[m, rows, :] = p * rbuf[m, rows, :] + q * ubuf[m, rows, :]
            return 0

        lax.fori_loop(0, rbuf.shape[1] // 8, row, 0, unroll=8)
        store(m).start()
    for m in range(2 * W):
        store(m).wait()


def density_kernel(coefs, core_ref, me_ref, *refs, count):
    ti, to, own_v, parts = refs[:count], refs[count : 2 * count], refs[2 * count : 2 * count + 2], refs[2 * count + 2 : -6]
    dens, t_all, own, dbuf, load_sems, sems = refs[-6:]
    parts = [own, *parts]
    core, me = core_ref[0], me_ref[0]
    loads = [[], []]
    for half, sources in enumerate((to, ti)):
        places = pl.ds(half * W, W)
        pairs = [(x, t_all.at[d, places]) for d, x in enumerate(sources)] + [(own_v[half], own.at[places])]
        loads[half] = [pltpu.make_async_copy(x, y, load_sems.at[half, i]) for i, (x, y) in enumerate(pairs)]
    for c in loads[0] + loads[1]:
        c.start()
    pq = [both_of(coefs, lax.rem(me - d + count, count), (8, own.shape[2])) for d in range(count)]
    pq = [(-4.0 * p, -4.0 * q) for p, q in pq]

    def store(m):
        return pltpu.make_async_copy(dbuf.at[m], dens.at[plane_of(m, core)], sems.at[m])

    for m in range(2 * W):
        if m % W == 0:
            for c in loads[m // W]:
                c.wait()

        def part(t, _, m=m):
            rows = rows_of(t)
            acc = None
            for d in range(count):
                term = pq[d][0] * t_all[d, m, rows, :] + pq[d][1] * parts[d][m, rows, :]
                acc = term if acc is None else acc + term
            dbuf[m, rows, :] = acc
            return 0

        lax.fori_loop(0, dbuf.shape[1] // 8, part, 0, unroll=2)
        store(m).start()
    for m in range(2 * W):
        store(m).wait()


def shift(value, axis, count, d):
    return lax.ppermute(value, axis, [(i, (i + d) % count) for i in range(count)])


def body(orbitals, potential, trial_potential, eigenvalues, frequency, *, norb, ngrid):
    _, nx, ny, nz = orbitals.shape
    half = pltpu.VMEM((W, ny, nz), F32)
    tile = jax.ShapeDtypeStruct((8, 128), F32)
    part = ny // norb
    whole = jax.ShapeDtypeStruct((2 * W, ny, nz), F32)
    piece = pltpu.VMEM((W, part, nz), F32)
    long_piece = pltpu.VMEM((2 * W, part, nz), F32)
    core = core_index().astype(jnp.int32).reshape(1)
    me = lax.axis_index("orb").astype(jnp.int32).reshape(1)
    mz = jnp.asarray(np.stack(circulant(nz)))
    my = jnp.asarray(np.stack(circulant(ny)))
    orbitals, trial_potential = in_hbm(orbitals), in_hbm(trial_potential)

    inner_pairs = [(i, i ^ 1) for i in range(ngrid)]
    outer_pairs = [(i, i + 1) for i in range(1, ngrid - 1, 2)]
    outer_pairs += [(j, i) for i, j in outer_pairs]

    def outer_swap(x):
        with jax.named_scope("outer_swap"):
            return in_vmem(lax.ppermute(x, "grid", outer_pairs))

    def inner_swap(x):
        with jax.named_scope("inner_swap"):
            return in_vmem(lax.ppermute(x, "grid", inner_pairs))

    def local(stage, fo, fi, hi, *after):
        parts_type = long_piece if stage == 2 else piece
        gi, po, out, own, kept, *parts = call(
            functools.partial(local_kernel, stage=stage, count=norb),
            (half, half, tile, in_hbm_type(piece), in_hbm_type(whole)) + (parts_type,) * (norb - 1),
            [VM] * 4 + [ANY, SM, SM, SM, VM, VM] + [ANY] * len(after),
            (VM, VM, VM, ANY, ANY) + (VM,) * (norb - 1),
            [
                pltpu.VMEM(half.shape, F32),
                pltpu.VMEM(piece.shape, F32),
                pltpu.VMEM(whole.shape, F32),
                pltpu.SemaphoreType.DMA((W,)),
                pltpu.SemaphoreType.DMA((3,)),
            ],
            limit=10,
        )(fo, fi, hi, potential, orbitals, eigenvalues, core, me, mz, my, *after)
        return gi, po, out, kept, [own, *parts]

    def add_halo(po, ho, *after):
        return call(halo_kernel, half, [VM, VM] + [VM] * len(after), VM, limit=4)(po, ho, *after)

    def send_parts(parts):
        with jax.named_scope("density_parts"):
            return [parts[0]] + [shift(parts[d], "orb", norb, d) for d in range(1, norb)]

    ro, ri = call(
        source_kernel,
        (half, half),
        [ANY, ANY, SM],
        (VM, VM),
        [pltpu.VMEM(whole.shape, F32), pltpu.VMEM(whole.shape, F32), pltpu.SemaphoreType.DMA((2, 2 * W))],
        limit=10,
    )(orbitals, trial_potential, core)
    ho = outer_swap(ro)
    ti, po, rr, r_kept, parts = local(0, ro, ri, inner_swap(ri))
    parts_ti = send_parts(parts)
    to = add_halo(po, ho)

    ho = outer_swap(to)
    ui, po, tt, t_kept, parts = local(1, to, ti, inner_swap(ti))
    parts_to = send_parts(parts)
    uo = add_halo(po, ho, *parts_ti[1:])

    ho = outer_swap(uo)
    vi, po, _, u_kept, parts = local(2, uo, ui, inner_swap(ui))
    shares, inner, to, orb_o = call(
        sums_kernel,
        (tile, jax.ShapeDtypeStruct((2, 8, 128), F32), half, half),
        [ANY] * 3 + [VM] * 5 + [SM],
        (VM,) * 4,
        [pltpu.VMEM(whole.shape, F32), pltpu.VMEM(half.shape, F32), pltpu.SemaphoreType.DMA((3 + W,))],
        limit=5,
    )(r_kept, t_kept, orbitals, uo, ui, vi, rr, tt, core)

    shares, own_vo, *parts_v = call(
        functools.partial(last_kernel, count=norb),
        (jax.ShapeDtypeStruct((ngrid, 8, 128), F32), in_hbm_type(piece)) + (long_piece,) * (norb - 1),
        [VM] * 6 + [SM] + [VM] * (2 * norb - 2),
        (VM, ANY) + (VM,) * (norb - 1),
        [pltpu.VMEM(piece.shape, F32), pltpu.SemaphoreType.DMA((1,))],
        limit=8,
    )(po, ho, to, orb_o, shares, inner, me, *parts[1:], *parts_to[1:])
    with jax.named_scope("density_parts"):
        parts_v = [in_vmem(shift(x, "orb", norb, d)) for d, x in enumerate(parts_v, 1)]
    with jax.named_scope("all_shares"):
        shares = lax.all_to_all(shares, "grid", 0, 0, tiled=True)
    coefs = call(coefficient_kernel, jax.ShapeDtypeStruct((norb, 8, 128), F32), [VM, SM], VM, limit=2)(
        shares, frequency
    )
    with jax.named_scope("all_coefficients"):
        all_coefs = lax.all_to_all(coefs, "orb", 0, 0, tiled=True)
    solution = call(
        solution_kernel,
        in_hbm_type(jax.ShapeDtypeStruct((1, nx, ny, nz), F32)),
        [ANY, ANY, VM, SM],
        ANY,
        [pltpu.VMEM(whole.shape, F32)] * 3 + [pltpu.SemaphoreType.DMA((2, nx)), pltpu.SemaphoreType.DMA((nx,))],
        limit=9,
    )(in_hbm(r_kept), in_hbm(u_kept), coefs, core)
    waiting = [in_hbm(x) for x in (*parts_ti, *parts_to, own_vo, parts[0])]
    density = call(
        functools.partial(density_kernel, count=norb),
        in_hbm_type(long_piece),
        [VM, SM, SM] + [ANY] * len(waiting) + [VM] * (norb - 1),
        ANY,
        [
            pltpu.VMEM((norb, *long_piece.shape), F32),
            pltpu.VMEM(long_piece.shape, F32),
            pltpu.VMEM(long_piece.shape, F32),
            pltpu.SemaphoreType.DMA((2, norb + 1)),
            pltpu.SemaphoreType.DMA((nx,)),
        ],
        limit=8,
    )(all_coefs, core, me, *waiting, *parts_v)
    return solution, density


def solution(mesh):
    in_specs = (
        P("orb", "grid", None, None),
        P("grid", None, None),
        P("grid", None, None),
        P("orb"),
        P(),
    )
    out_specs = (P("orb", "grid", None, None), P("grid", "orb", None))
    step = functools.partial(body, norb=mesh.shape["orb"], ngrid=mesh.shape["grid"])
    return jax.shard_map(step, mesh=mesh, in_specs=in_specs, out_specs=out_specs, check_vma=False)
```

time: 455 us -> 114 us (0.25)
  the two profiles are of different devices: /device:TPU:7 before, /device:TPU:8 now
where the time goes in v1:
time: 114 us; the launch traced here: 113 us
  starting transfers between devices  54.6 us (48%)
  Pallas kernels  42.2 us (37%)
  waiting for transfers between devices  13.2 us (12%)
  between operations  2.24 us (2%)
    all_to_all x1, starting transfers between devices, body(): shares = lax.all_to_all(shares, 'grid', 0, 0, tiled=True)  24.2 us
    pallas_call x3, Pallas kernels, local(): call(functools.partial(local_kernel, stage=stage, count=norb), (half, hal...  22.5 us
    ppermute x9, starting transfers between devices, shift(): lax.ppermute(value, axis, [(i, (i + d) % count) for i in range(count)])  14.6 us
    all_to_all x1, waiting for transfers between devices, body(): shares = lax.all_to_all(shares, 'grid', 0, 0, tiled=True)  12.3 us
    ppermute x3, starting transfers between devices, inner_swap(): return in_vmem(lax.ppermute(x, 'grid', inner_pairs))  8.1 us
    pallas_call x1, Pallas kernels, body(): call(solution_kernel, in_hbm_type(jax.ShapeDtypeStruct((1, nx, ny, nz), F...  4.76 us
    all_to_all x1, starting transfers between devices, body(): all_coefs = lax.all_to_all(coefs, 'orb', 0, 0, tiled=True)  4.56 us
    pallas_call x1, Pallas kernels, body(): call(source_kernel, (half, half), [ANY, ANY, SM], (VM, VM), [pltpu.VMEM(w...  4.16 us
  transfers between devices with their start and end apart: 17, of which 2 were waited for; matrix products, arithmetic and copies ran while one was open for 0% of the time, Pallas kernels for 29%

profile of v1, /device:TPU:8, one launch (start us, length us, event | category | flops | bytes accessed | tf_op | source)
XLA Modules:
  0.0 112.6 jit_solution(1991643323309794341)
XLA Ops:
  0.7 4.2 %shard_map.86 = (f32[6,192,256]{2,1,0:T(8,128)}, f32[6,192,256]{2,1,0:T(8,128)}) custom-call(f32[1,12,192,256]{3,2,1,0:T(8,128)} %orb.9, f32[12,192,256]{2,1,0:T(8,128)} %trial.1, s32[1]{0:T(128)} %bitcast.core_ref), custom_call_target="tpu_custom_call" | custom-call | tf_op jit(solution)/shard_map/pallas_call | solution.py:450
  4.9 1.7 %collective-permute-start.1 = (f32[6,192,256]{2,1,0:T(8,128)}, f32[6,192,256]{2,1,0:T(8,128)}, u32[]{:S(2)}, u32[]{:S(2)}) collective-permute-start(f32[6,192,256]{2,1,0:T(8,128)} %get-tuple-element.36.fo), channel_id=1, source_target_pairs={{1,2},{3,4},{5,6},{7,8},{9,10},{11,12},{13,14},{15,16},{17,18},{19... | collective-permute-start | bytes 3538952 | tf_op jit(solution)/shard_map/outer_swap/ppermute | solution.py:419
  7.3 0.8 collective-permute-done.hi_halo
  8.1 8.7 %shard_map.87 = (f32[6,192,256]{2,1,0:T(8,128)S(1)}, f32[6,192,256]{2,1,0:T(8,128)S(1)}, f32[8,128]{1,0:T(8,128)S(1)}, f32[6,48,256]{2,1,0:T(8,128)}, f32[12,192...) custom-call(f32[6,192,256]{2,1,0:T(8,128)} %get-tuple-element.36.fo, ...), custom_call_target="tpu_custom_call" | custom-call | tf_op jit(solution)/shard_map/pallas_call | solution.py:427
  16.8 1.1 collective-permute-start.2
  17.9 1.7 %shard_map.88.fo = f32[6,192,256]{2,1,0:T(8,128)S(1)} custom-call(f32[6,192,256]{2,1,0:T(8,128)S(1)} %get-tuple-element.39.po, f32[6,192,256]{2,1,0:T(8,128)} %collective-permute-done.1.ho), custom_call_target="tpu_custom_call" | custom-call | tf_op jit(solution)/shard_map/pallas_call | solution.py:444
  20.4 1.7 %collective-permute-start.4 = (f32[6,48,256]{2,1,0:T(8,128)S(1)}, f32[6,48,256]{2,1,0:T(8,128)S(1)}, u32[]{:S(2)}, u32[]{:S(2)}) collective-permute-start(f32[6,48,256]{2,1,0:T(8,128)S(1)} %get-tuple-element.42), channel_id=1, source_target_pairs={{0,64},{64,128},{128,192},{192,0},{1,65},{65,129},{129,193},{193,1... | collective-permute-start | bytes 884744 | tf_op jit(solution)/shard_map/density_parts/ppermute | solution.py:396
  22.0 1.8 %collective-permute-start.5 = (f32[6,48,256]{2,1,0:T(8,128)S(1)}, f32[6,48,256]{2,1,0:T(8,128)S(1)}, u32[]{:S(2)}, u32[]{:S(2)}) collective-permute-start(f32[6,48,256]{2,1,0:T(8,128)S(1)} %get-tuple-element.43), channel_id=1, source_target_pairs={{0,128},{64,192},{128,0},{192,64},{1,129},{65,193},{129,1},{193,65... | collective-permute-start | bytes 884744 | tf_op jit(solution)/shard_map/density_parts/ppermute | solution.py:396
  23.8 1.6 %collective-permute-start.6 = (f32[6,48,256]{2,1,0:T(8,128)S(1)}, f32[6,48,256]{2,1,0:T(8,128)S(1)}, u32[]{:S(2)}, u32[]{:S(2)}) collective-permute-start(f32[6,48,256]{2,1,0:T(8,128)S(1)} %get-tuple-element.44), channel_id=1, source_target_pairs={{0,192},{64,0},{128,64},{192,128},{1,193},{65,1},{129,65},{193,129... | collective-permute-start | bytes 884744 | tf_op jit(solution)/shard_map/density_parts/ppermute | solution.py:396
  25.4 6.7 %shard_map.89 = (f32[6,192,256]{2,1,0:T(8,128)S(1)}, f32[6,192,256]{2,1,0:T(8,128)S(1)}, f32[8,128]{1,0:T(8,128)S(1)}, f32[6,48,256]{2,1,0:T(8,128)}, f32[12,192...) custom-call(f32[6,192,256]{2,1,0:T(8,128)S(1)} %shard_map.88.fo, ...), custom_call_target="tpu_custom_call" | custom-call | tf_op jit(solution)/shard_map/pallas_call | solution.py:427
  32.1 6.9 %collective-permute-start.7 = (f32[6,192,256]{2,1,0:T(8,128)S(1)}, f32[6,192,256]{2,1,0:T(8,128)S(1)}, u32[]{:S(2)}, u32[]{:S(2)}) collective-permute-start(f32[6,192,256]{2,1,0:T(8,128)S(1)} %get-tuple-element.45.fi.ui), channel_id=1, source_target_pairs={{0,1},{1,0},{2,3},{3,2},{4,5},{5,4},{6,7},{7,6},{8,9},{9,8},{10,11... | collective-permute-start | bytes 3538952 | tf_op jit(solution)/shard_map/inner_swap/ppermute | solution.py:423
  41.2 1.8 %collective-permute-start.11 = (f32[6,48,256]{2,1,0:T(8,128)S(1)}, f32[6,48,256]{2,1,0:T(8,128)S(1)}, u32[]{:S(2)}, u32[]{:S(2)}) collective-permute-start(f32[6,48,256]{2,1,0:T(8,128)S(1)} %get-tuple-element.61), channel_id=1, source_target_pairs={{0,192},{64,0},{128,64},{192,128},{1,193},{65,1},{129,65},{193,129... | collective-permute-start | bytes 884744 | tf_op jit(solution)/shard_map/density_parts/ppermute | solution.py:396
  43.6 7.1 %shard_map.91 = (f32[6,192,256]{2,1,0:T(8,128)S(1)}, f32[6,192,256]{2,1,0:T(8,128)S(1)}, f32[8,128]{1,0:T(8,128)}, f32[6,48,256]{2,1,0:T(8,128)}, f32[12,192,256...) custom-call(f32[6,192,256]{2,1,0:T(8,128)S(1)} %shard_map.90.fo.uo, ...), custom_call_target="tpu_custom_call" | custom-call | tf_op jit(solution)/shard_map/pallas_call | solution.py:427
  50.7 2.7 %shard_map.92 = (f32[8,128]{1,0:T(8,128)S(1)}, f32[2,8,128]{2,1,0:T(8,128)S(1)}, f32[6,192,256]{2,1,0:T(8,128)S(1)}, f32[6,192,256]{2,1,0:T(8,128)S(1)}) custom-call(f32[12,192,256]{2,1,0:T(8,128)S(1)} %copy-done.1, f32[12,192,256]{2,1,0:T(8,128)S(1)} %copy-done.3, f32[1,12,192,256]{3,2,1,0:T(8,128)} %orb.9, f32[6,192,256]{2,1,0:T(8,128)S(1)} %shard_map.90.fo.uo, ...), custom_call_target="tpu_custom_call" | custom-call | tf_op jit(solution)/shard_map/pallas_call | solution.py:470
  53.5 2.2 %shard_map.93 = (f32[64,8,128]{2,1,0:T(8,128)}, f32[6,48,256]{2,1,0:T(8,128)}, f32[12,48,256]{2,1,0:T(8,128)}, f32[12,48,256]{2,1,0:T(8,128)}, f32[12,48,256]{2,1,0:T(8,128)S(1)}) custom-call(f32[6,192,256]{2,1,0:T(8,128)S(1)} %get-tuple-element.47.po, f32[6,192,256]{2,1,0:T(8,128)S(1)} %collective-permute-done.8.ho, ...), custom_call_target="tpu_custom_call" | custom-call | tf_op jit(solution)/shard_map/pallas_call | solution.py:479
  55.7 2.1 %collective-permute-start.12 = (f32[12,48,256]{2,1,0:T(8,128)}, f32[12,48,256]{2,1,0:T(8,128)S(1)}, u32[]{:S(2)}, u32[]{:S(2)}) collective-permute-start(f32[12,48,256]{2,1,0:T(8,128)} %get-tuple-element.67), channel_id=1, source_target_pairs={{0,64},{64,128},{128,192},{192,0},{1,65},{65,129},{129,193},{193,1... | collective-permute-start | bytes 1769480 | tf_op jit(solution)/shard_map/density_parts/ppermute | solution.py:396
  57.8 2.0 %collective-permute-start.13 = (f32[12,48,256]{2,1,0:T(8,128)}, f32[12,48,256]{2,1,0:T(8,128)S(1)}, u32[]{:S(2)}, u32[]{:S(2)}) collective-permute-start(f32[12,48,256]{2,1,0:T(8,128)} %get-tuple-element.68), channel_id=1, source_target_pairs={{0,128},{64,192},{128,0},{192,64},{1,129},{65,193},{129,1},{193,65... | collective-permute-start | bytes 1769480 | tf_op jit(solution)/shard_map/density_parts/ppermute | solution.py:396
  59.9 2.5 %collective-permute-start.14 = (f32[12,48,256]{2,1,0:T(8,128)S(1)}, f32[12,48,256]{2,1,0:T(8,128)S(1)}, u32[]{:S(2)}, u32[]{:S(2)}) collective-permute-start(f32[12,48,256]{2,1,0:T(8,128)S(1)} %get-tuple-element.69), channel_id=1, source_target_pairs={{0,192},{64,0},{128,64},{192,128},{1,193},{65,1},{129,65},{193,129... | collective-permute-start | bytes 1769480 | tf_op jit(solution)/shard_map/density_parts/ppermute | solution.py:396
  62.4 24.2 %all-to-all-start = ((f32[64,8,128]{2,1,0:T(8,128)}), f32[64,8,128]{2,1,0:T(8,128)S(1)}, u32[]{:S(2)}, u32[]{:S(2)}) async-start(f32[64,8,128]{2,1,0:T(8,128)} %get-tuple-element.62), calls=%async_computation | async-start | bytes 524288 | tf_op jit(solution)/shard_map/all_shares/all_to_all | solution.py:490
  87.2 12.3 %all-to-all-done.shares = f32[64,8,128]{2,1,0:T(8,128)S(1)} async-done(((f32[64,8,128]{2,1,0:T(8,128)}), f32[64,8,128]{2,1,0:T(8,128)S(1)}, u32[]{:S(2)}, u32[]{:S(2)}) %all-to-all-start) | async-done | bytes 262176 | tf_op jit(solution)/shard_map/all_shares/all_to_all | solution.py:490
  99.6 0.9 shard_map.94.coefs
  100.4 4.6 %all-to-all-start.1 = ((f32[4,8,128]{2,1,0:T(8,128)}), f32[4,8,128]{2,1,0:T(8,128)S(1)}, u32[]{:S(2)}, u32[]{:S(2)}) async-start(f32[4,8,128]{2,1,0:T(8,128)} %shard_map.94.coefs), calls=%async_computation.1 | async-start | bytes 32768 | tf_op jit(solution)/shard_map/all_coefficients/all_to_all | solution.py:495
  105.0 4.8 %shard_map.95 = f32[1,12,192,256]{3,2,1,0:T(8,128)} custom-call(f32[12,192,256]{2,1,0:T(8,128)} %get-tuple-element.38.r, f32[12,192,256]{2,1,0:T(8,128)} %get-tuple-element.46.u, f32[4,8,128]{2,1,0:T(8,128)} %shard_map.94.coefs, s32[1]{0:T(128)} %bitcast.core_ref), custom_call_target="tpu_custom_call" | custom-call | tf_op jit(solution)/shard_map/pallas_call | solution.py:496
  109.8 2.9 %shard_map.96 = f32[12,48,256]{2,1,0:T(8,128)} custom-call(f32[4,8,128]{2,1,0:T(8,128)S(1)} %all-to-all-done.1.coefs, s32[1]{0:T(128)} %bitcast.core_ref, s32[1]{0:T(128)} %bitcast.1.me_ref, f32[6,48,256]{2,1,0:T(8,128)} %get-tuple-element.63.refs_0_, f32[6,48,256]{2,1,0:T(8,128)} %copy-done.5, f32[6,48,256]{2,1,0:T(8,128)} %copy-done.6, ...), custom_call_target="tpu_custom_call" | custom-call | tf_op jit(solution)/shard_map/pallas_call | solution.py:505
  (43 shorter events, 3.6 us)
Async XLA Ops:
  0.6 7.5 %copy-start = (f32[12,192,256]{2,1,0:T(8,128)S(1)}, f32[12,192,256]{2,1,0:T(8,128)}, u32[]{:S(2)}) copy-start(f32[12,192,256]{2,1,0:T(8,128)} %pot.5) | copy-start | bytes 7077892
  0.6 7.5 %copy-start.2 = (bf16[2,256,256]{2,1,0:T(8,128)(2,1)S(1)}, bf16[2,256,256]{2,1,0:T(8,128)(2,1)}, u32[]{:S(2)}) copy-start(bf16[2,256,256]{2,1,0:T(8,128)(2,1)} %constant.18.clone.mz) | copy-start | bytes 786436
  0.7 7.5 %copy-start.4 = (bf16[2,192,192]{2,1,0:T(8,128)(2,1)S(1)}, bf16[2,192,192]{2,1,0:T(8,128)(2,1)}, u32[]{:S(2)}) copy-start(bf16[2,192,192]{2,1,0:T(8,128)(2,1)} %constant.19.clone.my) | copy-start | bytes 442372
  4.8 3.3 %collective-permute-start = (f32[6,192,256]{2,1,0:T(8,128)}, f32[6,192,256]{2,1,0:T(8,128)}, u32[]{:S(2)}, u32[]{:S(2)}) collective-permute-start(f32[6,192,256]{2,1,0:T(8,128)} %get-tuple-element.37.fi), channel_id=1, source_target_pairs={{0,1},{1,0},{2,3},{3,2},{4,5},{5,4},{6,7},{7,6},{8,9},{9,8},{10,11... | collective-permute-start | bytes 3538952 | tf_op jit(solution)/shard_map/inner_swap/ppermute | solution.py:423
  4.9 13.0 %collective-permute-start.1 = (f32[6,192,256]{2,1,0:T(8,128)}, f32[6,192,256]{2,1,0:T(8,128)}, u32[]{:S(2)}, u32[]{:S(2)}) collective-permute-start(f32[6,192,256]{2,1,0:T(8,128)} %get-tuple-element.36.fo), channel_id=1, source_target_pairs={{1,2},{3,4},{5,6},{7,8},{9,10},{11,12},{13,14},{15,16},{17,18},{19... | collective-permute-start | bytes 3538952 | tf_op jit(solution)/shard_map/outer_swap/ppermute | solution.py:419
  16.8 8.6 %collective-permute-start.2 = (f32[6,192,256]{2,1,0:T(8,128)S(1)}, f32[6,192,256]{2,1,0:T(8,128)S(1)}, u32[]{:S(2)}, u32[]{:S(2)}) collective-permute-start(f32[6,192,256]{2,1,0:T(8,128)S(1)} %get-tuple-element.40.fi), channel_id=1, source_target_pairs={{0,1},{1,0},{2,3},{3,2},{4,5},{5,4},{6,7},{7,6},{8,9},{9,8},{10,11... | collective-permute-start | bytes 3538952 | tf_op jit(solution)/shard_map/inner_swap/ppermute | solution.py:423
  19.6 19.4 %collective-permute-start.3 = (f32[6,192,256]{2,1,0:T(8,128)S(1)}, f32[6,192,256]{2,1,0:T(8,128)S(1)}, u32[]{:S(2)}, u32[]{:S(2)}) collective-permute-start(f32[6,192,256]{2,1,0:T(8,128)S(1)} %shard_map.88.fo), channel_id=1, source_target_pairs={{1,2},{3,4},{5,6},{7,8},{9,10},{11,12},{13,14},{15,16},{17,18},{19... | collective-permute-start | bytes 3538952 | tf_op jit(solution)/shard_map/outer_swap/ppermute | solution.py:419
  20.4 18.6 %collective-permute-start.4 = (f32[6,48,256]{2,1,0:T(8,128)S(1)}, f32[6,48,256]{2,1,0:T(8,128)S(1)}, u32[]{:S(2)}, u32[]{:S(2)}) collective-permute-start(f32[6,48,256]{2,1,0:T(8,128)S(1)} %get-tuple-element.42), channel_id=1, source_target_pairs={{0,64},{64,128},{128,192},{192,0},{1,65},{65,129},{129,193},{193,1... | collective-permute-start | bytes 884744 | tf_op jit(solution)/shard_map/density_parts/ppermute | solution.py:396
  22.0 17.0 %collective-permute-start.5 = (f32[6,48,256]{2,1,0:T(8,128)S(1)}, f32[6,48,256]{2,1,0:T(8,128)S(1)}, u32[]{:S(2)}, u32[]{:S(2)}) collective-permute-start(f32[6,48,256]{2,1,0:T(8,128)S(1)} %get-tuple-element.43), channel_id=1, source_target_pairs={{0,128},{64,192},{128,0},{192,64},{1,129},{65,193},{129,1},{193,65... | collective-permute-start | bytes 884744 | tf_op jit(solution)/shard_map/density_parts/ppermute | solution.py:396
  23.8 15.2 %collective-permute-start.6 = (f32[6,48,256]{2,1,0:T(8,128)S(1)}, f32[6,48,256]{2,1,0:T(8,128)S(1)}, u32[]{:S(2)}, u32[]{:S(2)}) collective-permute-start(f32[6,48,256]{2,1,0:T(8,128)S(1)} %get-tuple-element.44), channel_id=1, source_target_pairs={{0,192},{64,0},{128,64},{192,128},{1,193},{65,1},{129,65},{193,129... | collective-permute-start | bytes 884744 | tf_op jit(solution)/shard_map/density_parts/ppermute | solution.py:396
  32.1 11.5 %collective-permute-start.7 = (f32[6,192,256]{2,1,0:T(8,128)S(1)}, f32[6,192,256]{2,1,0:T(8,128)S(1)}, u32[]{:S(2)}, u32[]{:S(2)}) collective-permute-start(f32[6,192,256]{2,1,0:T(8,128)S(1)} %get-tuple-element.45.fi.ui), channel_id=1, source_target_pairs={{0,1},{1,0},{2,3},{3,2},{4,5},{5,4},{6,7},{7,6},{8,9},{9,8},{10,11... | collective-permute-start | bytes 3538952 | tf_op jit(solution)/shard_map/inner_swap/ppermute | solution.py:423
  39.9 13.6 %collective-permute-start.8 = (f32[6,192,256]{2,1,0:T(8,128)S(1)}, f32[6,192,256]{2,1,0:T(8,128)S(1)}, u32[]{:S(2)}, u32[]{:S(2)}) collective-permute-start(f32[6,192,256]{2,1,0:T(8,128)S(1)} %shard_map.90.fo.uo), channel_id=1, source_target_pairs={{1,2},{3,4},{5,6},{7,8},{9,10},{11,12},{13,14},{15,16},{17,18},{19... | collective-permute-start | bytes 3538952 | tf_op jit(solution)/shard_map/outer_swap/ppermute | solution.py:419
  40.7 12.8 %collective-permute-start.10 = (f32[6,48,256]{2,1,0:T(8,128)S(1)}, f32[6,48,256]{2,1,0:T(8,128)S(1)}, u32[]{:S(2)}, u32[]{:S(2)}) collective-permute-start(f32[6,48,256]{2,1,0:T(8,128)S(1)} %get-tuple-element.60), channel_id=1, source_target_pairs={{0,128},{64,192},{128,0},{192,64},{1,129},{65,193},{129,1},{193,65... | collective-permute-start | bytes 884744 | tf_op jit(solution)/shard_map/density_parts/ppermute | solution.py:396
  41.2 12.3 %collective-permute-start.11 = (f32[6,48,256]{2,1,0:T(8,128)S(1)}, f32[6,48,256]{2,1,0:T(8,128)S(1)}, u32[]{:S(2)}, u32[]{:S(2)}) collective-permute-start(f32[6,48,256]{2,1,0:T(8,128)S(1)} %get-tuple-element.61), channel_id=1, source_target_pairs={{0,192},{64,0},{128,64},{192,128},{1,193},{65,1},{129,65},{193,129... | collective-permute-start | bytes 884744 | tf_op jit(solution)/shard_map/density_parts/ppermute | solution.py:396
  43.1 10.4 %collective-permute-start.9 = (f32[6,48,256]{2,1,0:T(8,128)S(1)}, f32[6,48,256]{2,1,0:T(8,128)S(1)}, u32[]{:S(2)}, u32[]{:S(2)}) collective-permute-start(f32[6,48,256]{2,1,0:T(8,128)S(1)} %get-tuple-element.59), channel_id=1, source_target_pairs={{0,64},{64,128},{128,192},{192,0},{1,65},{65,129},{129,193},{193,1... | collective-permute-start | bytes 884744 | tf_op jit(solution)/shard_map/density_parts/ppermute | solution.py:396
  43.6 7.2 %copy-start.1 = (f32[12,192,256]{2,1,0:T(8,128)S(1)}, f32[12,192,256]{2,1,0:T(8,128)}, u32[]{:S(2)}) copy-start(f32[12,192,256]{2,1,0:T(8,128)} %get-tuple-element.38.r) | copy-start | bytes 7077892
  43.6 7.2 %copy-start.3 = (f32[12,192,256]{2,1,0:T(8,128)S(1)}, f32[12,192,256]{2,1,0:T(8,128)}, u32[]{:S(2)}) copy-start(f32[12,192,256]{2,1,0:T(8,128)} %get-tuple-element.48.t_kept) | copy-start | bytes 7077892
  53.5 2.2 %copy-start.8 = (f32[6,48,256]{2,1,0:T(8,128)}, f32[6,48,256]{2,1,0:T(8,128)S(1)}, u32[]{:S(2)}) copy-start(f32[6,48,256]{2,1,0:T(8,128)S(1)} %collective-permute-done.10.refs_4_.refs_6_) | copy-start | bytes 884740
  53.5 2.2 %copy-start.9 = (f32[6,48,256]{2,1,0:T(8,128)}, f32[6,48,256]{2,1,0:T(8,128)S(1)}, u32[]{:S(2)}) copy-start(f32[6,48,256]{2,1,0:T(8,128)S(1)} %collective-permute-done.11.refs_5_.refs_7_) | copy-start | bytes 884740
  55.7 54.0 %collective-permute-start.12 = (f32[12,48,256]{2,1,0:T(8,128)}, f32[12,48,256]{2,1,0:T(8,128)S(1)}, u32[]{:S(2)}, u32[]{:S(2)}) collective-permute-start(f32[12,48,256]{2,1,0:T(8,128)} %get-tuple-element.67), channel_id=1, source_target_pairs={{0,64},{64,128},{128,192},{192,0},{1,65},{65,129},{129,193},{193,1... | collective-permute-start | bytes 1769480 | tf_op jit(solution)/shard_map/density_parts/ppermute | solution.py:396
  57.8 51.9 %collective-permute-start.13 = (f32[12,48,256]{2,1,0:T(8,128)}, f32[12,48,256]{2,1,0:T(8,128)S(1)}, u32[]{:S(2)}, u32[]{:S(2)}) collective-permute-start(f32[12,48,256]{2,1,0:T(8,128)} %get-tuple-element.68), channel_id=1, source_target_pairs={{0,128},{64,192},{128,0},{192,64},{1,129},{65,193},{129,1},{193,65... | collective-permute-start | bytes 1769480 | tf_op jit(solution)/shard_map/density_parts/ppermute | solution.py:396
  59.9 49.9 %collective-permute-start.14 = (f32[12,48,256]{2,1,0:T(8,128)S(1)}, f32[12,48,256]{2,1,0:T(8,128)S(1)}, u32[]{:S(2)}, u32[]{:S(2)}) collective-permute-start(f32[12,48,256]{2,1,0:T(8,128)S(1)} %get-tuple-element.69), channel_id=1, source_target_pairs={{0,192},{64,0},{128,64},{192,128},{1,193},{65,1},{129,65},{193,129... | collective-permute-start | bytes 1769480 | tf_op jit(solution)/shard_map/density_parts/ppermute | solution.py:396
  62.4 37.2 %all-to-all-start = ((f32[64,8,128]{2,1,0:T(8,128)}), f32[64,8,128]{2,1,0:T(8,128)S(1)}, u32[]{:S(2)}, u32[]{:S(2)}) async-start(f32[64,8,128]{2,1,0:T(8,128)} %get-tuple-element.62), calls=%async_computation | async-start | bytes 524288 | tf_op jit(solution)/shard_map/all_shares/all_to_all | solution.py:490
  100.4 9.3 %all-to-all-start.1 = ((f32[4,8,128]{2,1,0:T(8,128)}), f32[4,8,128]{2,1,0:T(8,128)S(1)}, u32[]{:S(2)}, u32[]{:S(2)}) async-start(f32[4,8,128]{2,1,0:T(8,128)} %shard_map.94.coefs), calls=%async_computation.1 | async-start | bytes 32768 | tf_op jit(solution)/shard_map/all_coefficients/all_to_all | solution.py:495
  (4 other events, 4.7 us)

commit v2 on v1

--- a/solution.py
+++ b/solution.py
@@ -26,6 +26,7 @@
 SM = pl.BlockSpec(memory_space=pltpu.SMEM)
 ANY = pl.BlockSpec(memory_space=pl.ANY)
 MIB = 1 << 20
+GRID = ("chip", "core")
 
 
 def in_hbm_type(array):
@@ -56,7 +57,7 @@
 
 
 def core_index():
-    return lax.rem(lax.axis_index("grid"), 2)
+    return lax.axis_index("core")
 
 
 def rows_of(t):
@@ -74,8 +75,8 @@
     )
 
 
-def source_kernel(orb, trial, core_ref, ro, ri, a, b, sems):
-    core = core_ref[0]
+def source_kernel(orb, trial, ro, ri, a, b, sems):
+    core = core_index()
 
     def copies(m):
         p = plane_of(m, core)
@@ -99,11 +100,11 @@
     return quarter * part
 
 
-def local_kernel(fo, fi, hi_halo, pot, orb, energy, core_ref, me_ref, mz, my, *refs, stage, count):
+def local_kernel(fo, fi, hi_halo, pot, orb, energy, mz, my, *refs, stage, count):
     gi, po, tile, own_out, kept, *parts = refs[-count - 9 : -5]
     orb_v, own, yz, sems, more_sems = refs[-5:]
     parts = [own, *parts]
-    core, me = core_ref[0], me_ref[0]
+    core, me = core_index(), lax.axis_index("orb")
     nz = fo.shape[2]
     part = own.shape[1]
     first = 0 if stage == 1 else W
@@ -206,9 +207,9 @@
     return jnp.broadcast_to(scalar, shape)
 
 
-def sums_kernel(r, t_kept, orb, uo, ui, vi, rr_tile, tt_tile, core_ref, *refs):
+def sums_kernel(r, t_kept, orb, uo, ui, vi, rr_tile, tt_tile, *refs):
     rows_out, inner, to, orb_o, r_v, ti, sems = refs[-7:]
-    core = core_ref[0]
+    core = core_index()
     ro, ri = r_v.at[pl.ds(0, W)], r_v.at[pl.ds(W, W)]
     loads = (
         pltpu.make_async_copy(r, r_v, sems.at[0]),
@@ -255,13 +256,13 @@
         c.wait()
 
 
-def last_kernel(po, ho, to, orb, rows_in, inner, me_ref, *refs, count):
+def last_kernel(po, ho, to, orb, rows_in, inner, *refs, count):
     tile, own_out, *outs, own, sem = refs[-count - 3 :]
     for done, out in zip(refs[: count - 1], outs):
         for m in range(W, 2 * W):
             out[m] = done[m]
     outs = [own, *outs]
-    me = me_ref[0]
+    me = lax.axis_index("orb")
     theta = broad(rows_in[4:5])
     part = outs[0].shape[1]
     accs = inner[0], inner[1]
@@ -290,14 +291,27 @@
         row = jnp.where(lane == i, broad(rows_in[i : i + 1]), row)
     for i, x in enumerate(accs):
         row = jnp.where(lane == 5 + i, broad(whole_sum(x)), row)
-    for i in range(tile.shape[0]):
-        tile[i] = row
+    tile[...] = row
     store_own.wait()
 
 
-def coefficient_kernel(shares, freq, out):
+def copies_kernel(row, other, out):
+    mine = lax.broadcasted_iota(jnp.int32, row.shape, 0) == core_index()
+    both = jnp.where(mine, row[...], other[...])
+    for i in range(out.shape[0]):
+        out[i] = both
+
+
+def preload_kernel(field, out, sem):
+    load = pltpu.make_async_copy(field, out, sem.at[0])
+    load.start()
+    load.wait()
+
+
+def coefficient_kernel(shares, freq, *refs):
+    out = refs[-1]
     w2 = freq[0] * freq[0]
-    share = shares[:, 0, :]
+    share = jnp.concatenate([shares[:, 0, :], shares[:, 1, :]], axis=0)
     rr, tt, s0, s1, own, t0, t1 = (share[:, i : i + 1] for i in range(7))
 
     def total(x):
@@ -323,42 +337,37 @@
     return tuple(broad(one[4 * i : 4 * i + 1, 0:1], shape) for i in range(2))
 
 
-def solution_kernel(r, u, coefs, core_ref, sol, rbuf, ubuf, xbuf, in_sems, out_sems):
-    core = core_ref[0]
-
-    def fields(m):
-        return (
-            pltpu.make_async_copy(r.at[m], rbuf.at[m], in_sems.at[0, m]),
-            pltpu.make_async_copy(u.at[m], ubuf.at[m], in_sems.at[1, m]),
-        )
+def solution_kernel(r, u, coefs, sol, rbuf, xbuf, in_sems, out_sems):
+    core = core_index()
+
+    def field(m):
+        return pltpu.make_async_copy(r.at[m], rbuf.at[m], in_sems.at[m])
 
     def store(m):
         return pltpu.make_async_copy(xbuf.at[m], sol.at[0, plane_of(m, core)], out_sems.at[m])
 
     for m in range(2 * W):
-        for c in fields(m):
-            c.start()
-    p, q = both_of(coefs, 0, (8, rbuf.shape[2]))
-    for m in range(2 * W):
-        for c in fields(m):
-            c.wait()
+        field(m).start()
+    p, q = both_of(coefs, 0, (8, r.shape[2]))
+    for m in range(2 * W):
+        field(m).wait()
 
         def row(t, _, m=m):
             rows = rows_of(t)
-            xbuf[m, rows, :] = p * rbuf[m, rows, :] + q * ubuf[m, rows, :]
+            xbuf[m, rows, :] = p * rbuf[m, rows, :] + q * u[m, rows, :]
             return 0
 
-        lax.fori_loop(0, rbuf.shape[1] // 8, row, 0, unroll=8)
+        lax.fori_loop(0, r.shape[1] // 8, row, 0, unroll=8)
         store(m).start()
     for m in range(2 * W):
         store(m).wait()
 
 
-def density_kernel(coefs, core_ref, me_ref, *refs, count):
+def density_kernel(coefs, *refs, count):
     ti, to, own_v, parts = refs[:count], refs[count : 2 * count], refs[2 * count : 2 * count + 2], refs[2 * count + 2 : -6]
     dens, t_all, own, dbuf, load_sems, sems = refs[-6:]
     parts = [own, *parts]
-    core, me = core_ref[0], me_ref[0]
+    core, me = core_index(), lax.axis_index("orb")
     loads = [[], []]
     for half, sources in enumerate((to, ti)):
         places = pl.ds(half * W, W)
@@ -404,8 +413,6 @@
     whole = jax.ShapeDtypeStruct((2 * W, ny, nz), F32)
     piece = pltpu.VMEM((W, part, nz), F32)
     long_piece = pltpu.VMEM((2 * W, part, nz), F32)
-    core = core_index().astype(jnp.int32).reshape(1)
-    me = lax.axis_index("orb").astype(jnp.int32).reshape(1)
     mz = jnp.asarray(np.stack(circulant(nz)))
     my = jnp.asarray(np.stack(circulant(ny)))
     orbitals, trial_potential = in_hbm(orbitals), in_hbm(trial_potential)
@@ -416,18 +423,18 @@
 
     def outer_swap(x):
         with jax.named_scope("outer_swap"):
-            return in_vmem(lax.ppermute(x, "grid", outer_pairs))
+            return in_vmem(lax.ppermute(x, GRID, outer_pairs))
 
     def inner_swap(x):
         with jax.named_scope("inner_swap"):
-            return in_vmem(lax.ppermute(x, "grid", inner_pairs))
+            return in_vmem(lax.ppermute(x, GRID, inner_pairs))
 
     def local(stage, fo, fi, hi, *after):
         parts_type = long_piece if stage == 2 else piece
         gi, po, out, own, kept, *parts = call(
             functools.partial(local_kernel, stage=stage, count=norb),
             (half, half, tile, in_hbm_type(piece), in_hbm_type(whole)) + (parts_type,) * (norb - 1),
-            [VM] * 4 + [ANY, SM, SM, SM, VM, VM] + [ANY] * len(after),
+            [VM] * 4 + [ANY, SM, VM, VM] + [ANY] * len(after),
             (VM, VM, VM, ANY, ANY) + (VM,) * (norb - 1),
             [
                 pltpu.VMEM(half.shape, F32),
@@ -436,8 +443,8 @@
                 pltpu.SemaphoreType.DMA((W,)),
                 pltpu.SemaphoreType.DMA((3,)),
             ],
-            limit=10,
-        )(fo, fi, hi, potential, orbitals, eigenvalues, core, me, mz, my, *after)
+            limit=12,
+        )(fo, fi, hi, potential, orbitals, eigenvalues, mz, my, *after)
         return gi, po, out, kept, [own, *parts]
 
     def add_halo(po, ho, *after):
@@ -450,11 +457,11 @@
     ro, ri = call(
         source_kernel,
         (half, half),
-        [ANY, ANY, SM],
+        [ANY, ANY],
         (VM, VM),
         [pltpu.VMEM(whole.shape, F32), pltpu.VMEM(whole.shape, F32), pltpu.SemaphoreType.DMA((2, 2 * W))],
         limit=10,
-    )(orbitals, trial_potential, core)
+    )(orbitals, trial_potential)
     ho = outer_swap(ro)
     ti, po, rr, r_kept, parts = local(0, ro, ri, inner_swap(ri))
     parts_ti = send_parts(parts)
@@ -470,42 +477,46 @@
     shares, inner, to, orb_o = call(
         sums_kernel,
         (tile, jax.ShapeDtypeStruct((2, 8, 128), F32), half, half),
-        [ANY] * 3 + [VM] * 5 + [SM],
+        [ANY] * 3 + [VM] * 5,
         (VM,) * 4,
         [pltpu.VMEM(whole.shape, F32), pltpu.VMEM(half.shape, F32), pltpu.SemaphoreType.DMA((3 + W,))],
         limit=5,
-    )(r_kept, t_kept, orbitals, uo, ui, vi, rr, tt, core)
+    )(r_kept, t_kept, orbitals, uo, ui, vi, rr, tt)
 
     shares, own_vo, *parts_v = call(
         functools.partial(last_kernel, count=norb),
-        (jax.ShapeDtypeStruct((ngrid, 8, 128), F32), in_hbm_type(piece)) + (long_piece,) * (norb - 1),
-        [VM] * 6 + [SM] + [VM] * (2 * norb - 2),
+        (tile, in_hbm_type(piece)) + (long_piece,) * (norb - 1),
+        [VM] * (4 + 2 * norb),
         (VM, ANY) + (VM,) * (norb - 1),
         [pltpu.VMEM(piece.shape, F32), pltpu.SemaphoreType.DMA((1,))],
         limit=8,
-    )(po, ho, to, orb_o, shares, inner, me, *parts[1:], *parts_to[1:])
+    )(po, ho, to, orb_o, shares, inner, *parts[1:], *parts_to[1:])
     with jax.named_scope("density_parts"):
         parts_v = [in_vmem(shift(x, "orb", norb, d)) for d, x in enumerate(parts_v, 1)]
     with jax.named_scope("all_shares"):
-        shares = lax.all_to_all(shares, "grid", 0, 0, tiled=True)
-    coefs = call(coefficient_kernel, jax.ShapeDtypeStruct((norb, 8, 128), F32), [VM, SM], VM, limit=2)(
-        shares, frequency
+        shares = call(
+            copies_kernel, jax.ShapeDtypeStruct((ngrid // 2, 8, 128), F32), [VM, VM], VM, limit=4
+        )(shares, lax.ppermute(shares, GRID, inner_pairs))
+        shares = lax.all_to_all(shares, "chip", 0, 0, tiled=True)
+    u_all = call(preload_kernel, whole, [ANY], VM, [pltpu.SemaphoreType.DMA((1,))], limit=4)(in_hbm(u_kept))
+    coefs = call(coefficient_kernel, jax.ShapeDtypeStruct((norb, 8, 128), F32), [VM, SM, VM], VM, limit=4)(
+        shares, frequency, u_all
     )
     with jax.named_scope("all_coefficients"):
         all_coefs = lax.all_to_all(coefs, "orb", 0, 0, tiled=True)
     solution = call(
         solution_kernel,
         in_hbm_type(jax.ShapeDtypeStruct((1, nx, ny, nz), F32)),
-        [ANY, ANY, VM, SM],
+        [ANY, VM, VM],
         ANY,
-        [pltpu.VMEM(whole.shape, F32)] * 3 + [pltpu.SemaphoreType.DMA((2, nx)), pltpu.SemaphoreType.DMA((nx,))],
+        [pltpu.VMEM(whole.shape, F32)] * 2 + [pltpu.SemaphoreType.DMA((nx,))] * 2,
         limit=9,
-    )(in_hbm(r_kept), in_hbm(u_kept), coefs, core)
+    )(in_hbm(r_kept), u_all, coefs)
     waiting = [in_hbm(x) for x in (*parts_ti, *parts_to, own_vo, parts[0])]
     density = call(
         functools.partial(density_kernel, count=norb),
         in_hbm_type(long_piece),
-        [VM, SM, SM] + [ANY] * len(waiting) + [VM] * (norb - 1),
+        [VM] + [ANY] * len(waiting) + [VM] * (norb - 1),
         ANY,
         [
             pltpu.VMEM((norb, *long_piece.shape), F32),
@@ -515,18 +526,20 @@
             pltpu.SemaphoreType.DMA((nx,)),
         ],
         limit=8,
-    )(all_coefs, core, me, *waiting, *parts_v)
+    )(all_coefs, *waiting, *parts_v)
     return solution, density
 
 
 def solution(mesh):
+    norb, ngrid = mesh.shape["orb"], mesh.shape["grid"]
+    mesh = jax.sharding.Mesh(mesh.devices.reshape(norb, ngrid // 2, 2), ("orb", *GRID))
     in_specs = (
-        P("orb", "grid", None, None),
-        P("grid", None, None),
-        P("grid", None, None),
+        P("orb", GRID, None, None),
+        P(GRID, None, None),
+        P(GRID, None, None),
         P("orb"),
         P(),
     )
-    out_specs = (P("orb", "grid", None, None), P("grid", "orb", None))
-    step = functools.partial(body, norb=mesh.shape["orb"], ngrid=mesh.shape["grid"])
+    out_specs = (P("orb", GRID, None, None), P(GRID, "orb", None))
+    step = functools.partial(body, norb=norb, ngrid=ngrid)
     return jax.shard_map(step, mesh=mesh, in_specs=in_specs, out_specs=out_specs, check_vma=False)

time: 114 us -> 111 us (0.974)
  waiting for transfers between devices: 13.2 us -> 11.2 us
  Pallas kernels: 42.2 us -> 40.7 us
    ppermute x6 -> x7, starting transfers between devices: 11.3 us -> 19.6 us  [the longest x3 10.1 us: inner_swap(): return in_vmem(lax.ppermute(x, GRID, inner_pairs))]
    all_to_all x1, starting transfers between devices: 24.2 us -> 16.6 us  [body(): shares = lax.all_to_all(shares, 'chip', 0, 0, tiled=True)]
    all_to_all x1, waiting for transfers between devices: 12.3 us -> 8.46 us  [body(): shares = lax.all_to_all(shares, 'chip', 0, 0, tiled=True)]
    pallas_call x3, Pallas kernels: 22.5 us -> 20.6 us  [local(): call(functools.partial(local_kernel, stage=stage, count=norb), (half, hal...]
    ppermute x6 -> x7, waiting for transfers between devices: 0.83 us -> 2.28 us  [the longest x3 1.45 us: inner_swap(): return in_vmem(lax.ppermute(x, GRID, inner_pairs))]
    pallas_call x1, Pallas kernels: 4.76 us -> 3.42 us  [body(): call(solution_kernel, in_hbm_type(jax.ShapeDtypeStruct((1, nx, ny, nz), F...]
    pallas_call x2, Pallas kernels: 2.13 us -> 0.86 us  [add_halo(): call(halo_kernel, half, [VM, VM] + [VM] * len(after), VM, limit=4)]
    pallas_call x2 -> x4, Pallas kernels: 6.33 us -> 7.38 us  [the longest x1 2.78 us: body(): call(source_kernel, (half, half), [ANY, ANY], (VM, VM), [pltpu.VMEM(whole...]
  transfers between devices with their start and end apart: 17 -> 18, of which waited for: 2 -> 4; matrix products, arithmetic and copies ran while one was open for 0% -> 0% of each run, Pallas kernels for 29% -> 29%
where the time goes in v2:
time: 111 us; the launch traced here: 110 us
  starting transfers between devices  55.4 us (50%)
  Pallas kernels  40.7 us (37%)
  waiting for transfers between devices  11.2 us (10%)
  between operations  2.22 us (2%)
    pallas_call x3, Pallas kernels, local(): call(functools.partial(local_kernel, stage=stage, count=norb), (half, hal...  20.6 us
    all_to_all x1, starting transfers between devices, body(): shares = lax.all_to_all(shares, 'chip', 0, 0, tiled=True)  16.6 us
    ppermute x9, starting transfers between devices, shift(): lax.ppermute(value, axis, [(i, (i + d) % count) for i in range(count)])  14.6 us
    ppermute x3, starting transfers between devices, inner_swap(): return in_vmem(lax.ppermute(x, GRID, inner_pairs))  10.1 us
    all_to_all x1, waiting for transfers between devices, body(): shares = lax.all_to_all(shares, 'chip', 0, 0, tiled=True)  8.46 us
    ppermute x1, starting transfers between devices, body(): lax.ppermute(shares, GRID, inner_pairs)  7.38 us
    all_to_all x1, starting transfers between devices, body(): all_coefs = lax.all_to_all(coefs, 'orb', 0, 0, tiled=True)  4.55 us
    pallas_call x1, Pallas kernels, body(): call(functools.partial(density_kernel, count=norb), in_hbm_type(long_piec...  3.92 us
  transfers between devices with their start and end apart: 18, of which 4 were waited for; matrix products, arithmetic and copies ran while one was open for 0% of the time, Pallas kernels for 29%

profile of v2, /device:TPU:8, one launch (start us, length us, event | category | flops | bytes accessed | tf_op | source)
XLA Modules:
  0.0 110.1 jit_solution(16386645992884577020)
XLA Ops:
  0.7 2.8 %shard_map.86 = (f32[6,192,256]{2,1,0:T(8,128)S(1)}, f32[6,192,256]{2,1,0:T(8,128)S(1)}) custom-call(f32[1,12,192,256]{3,2,1,0:T(8,128)} %orb.9, f32[12,192,256]{2,1,0:T(8,128)} %trial.1), custom_call_target="tpu_custom_call" | custom-call | tf_op jit(solution)/shard_map/pallas_call | solution.py:457
  4.9 1.4 %collective-permute-done.hi_halo = f32[6,192,256]{2,1,0:T(8,128)S(1)} collective-permute-done((f32[6,192,256]{2,1,0:T(8,128)S(1)}, f32[6,192,256]{2,1,0:T(8,128)S(1)}, u32[]{:S(2)}, u32[]{:S(2)}) %collective-permute-start) | collective-permute-done | bytes 1179680 | tf_op jit(solution)/shard_map/inner_swap/ppermute | solution.py:430
  6.4 6.7 %shard_map.87 = (f32[6,192,256]{2,1,0:T(8,128)S(1)}, f32[6,192,256]{2,1,0:T(8,128)S(1)}, f32[8,128]{1,0:T(8,128)S(1)}, f32[6,48,256]{2,1,0:T(8,128)}, f32[12,192...) custom-call(f32[6,192,256]{2,1,0:T(8,128)S(1)} %get-tuple-element.36.fo, ...), custom_call_target="tpu_custom_call" | custom-call | tf_op jit(solution)/shard_map/pallas_call | solution.py:434
  13.1 1.5 %collective-permute-start.2 = (f32[6,192,256]{2,1,0:T(8,128)S(1)}, f32[6,192,256]{2,1,0:T(8,128)S(1)}, u32[]{:S(2)}, u32[]{:S(2)}) collective-permute-start(f32[6,192,256]{2,1,0:T(8,128)S(1)} %get-tuple-element.40.fi), channel_id=1, source_target_pairs={{0,1},{1,0},{2,3},{3,2},{4,5},{5,4},{6,7},{7,6},{8,9},{9,8},{10,11... | collective-permute-start | bytes 3538952 | tf_op jit(solution)/shard_map/inner_swap/ppermute | solution.py:430
  15.8 1.7 %collective-permute-start.4 = (f32[6,48,256]{2,1,0:T(8,128)S(1)}, f32[6,48,256]{2,1,0:T(8,128)S(1)}, u32[]{:S(2)}, u32[]{:S(2)}) collective-permute-start(f32[6,48,256]{2,1,0:T(8,128)S(1)} %get-tuple-element.42), channel_id=1, source_target_pairs={{0,64},{64,128},{128,192},{192,0},{1,65},{65,129},{129,193},{193,1... | collective-permute-start | bytes 884744 | tf_op jit(solution)/shard_map/density_parts/ppermute | solution.py:405
  17.4 1.6 %collective-permute-start.5 = (f32[6,48,256]{2,1,0:T(8,128)S(1)}, f32[6,48,256]{2,1,0:T(8,128)S(1)}, u32[]{:S(2)}, u32[]{:S(2)}) collective-permute-start(f32[6,48,256]{2,1,0:T(8,128)S(1)} %get-tuple-element.43), channel_id=1, source_target_pairs={{0,128},{64,192},{128,0},{192,64},{1,129},{65,193},{129,1},{193,65... | collective-permute-start | bytes 884744 | tf_op jit(solution)/shard_map/density_parts/ppermute | solution.py:405
  19.0 1.8 %collective-permute-start.6 = (f32[6,48,256]{2,1,0:T(8,128)S(1)}, f32[6,48,256]{2,1,0:T(8,128)S(1)}, u32[]{:S(2)}, u32[]{:S(2)}) collective-permute-start(f32[6,48,256]{2,1,0:T(8,128)S(1)} %get-tuple-element.44), channel_id=1, source_target_pairs={{0,192},{64,0},{128,64},{192,128},{1,193},{65,1},{129,65},{193,129... | collective-permute-start | bytes 884744 | tf_op jit(solution)/shard_map/density_parts/ppermute | solution.py:405
  20.8 6.7 %shard_map.89 = (f32[6,192,256]{2,1,0:T(8,128)S(1)}, f32[6,192,256]{2,1,0:T(8,128)S(1)}, f32[8,128]{1,0:T(8,128)S(1)}, f32[6,48,256]{2,1,0:T(8,128)}, f32[12,192...) custom-call(f32[6,192,256]{2,1,0:T(8,128)S(1)} %shard_map.88.fo, ...), custom_call_target="tpu_custom_call" | custom-call | tf_op jit(solution)/shard_map/pallas_call | solution.py:434
  27.5 8.5 %collective-permute-start.7 = (f32[6,192,256]{2,1,0:T(8,128)S(1)}, f32[6,192,256]{2,1,0:T(8,128)S(1)}, u32[]{:S(2)}, u32[]{:S(2)}) collective-permute-start(f32[6,192,256]{2,1,0:T(8,128)S(1)} %get-tuple-element.45.fi.ui), channel_id=1, source_target_pairs={{0,1},{1,0},{2,3},{3,2},{4,5},{5,4},{6,7},{7,6},{8,9},{9,8},{10,11... | collective-permute-start | bytes 3538952 | tf_op jit(solution)/shard_map/inner_swap/ppermute | solution.py:430
  38.2 2.1 %collective-permute-start.11 = (f32[6,48,256]{2,1,0:T(8,128)S(1)}, f32[6,48,256]{2,1,0:T(8,128)S(1)}, u32[]{:S(2)}, u32[]{:S(2)}) collective-permute-start(f32[6,48,256]{2,1,0:T(8,128)S(1)} %get-tuple-element.61), channel_id=1, source_target_pairs={{0,192},{64,0},{128,64},{192,128},{1,193},{65,1},{129,65},{193,129... | collective-permute-start | bytes 884744 | tf_op jit(solution)/shard_map/density_parts/ppermute | solution.py:405
  40.6 7.2 %shard_map.91 = (f32[6,192,256]{2,1,0:T(8,128)S(1)}, f32[6,192,256]{2,1,0:T(8,128)S(1)}, f32[8,128]{1,0:T(8,128)}, f32[6,48,256]{2,1,0:T(8,128)}, f32[12,192,256...) custom-call(f32[6,192,256]{2,1,0:T(8,128)S(1)} %shard_map.90.fo.uo, ...), custom_call_target="tpu_custom_call" | custom-call | tf_op jit(solution)/shard_map/pallas_call | solution.py:434
  47.8 2.7 %shard_map.93 = (f32[8,128]{1,0:T(8,128)S(1)}, f32[2,8,128]{2,1,0:T(8,128)S(1)}, f32[6,192,256]{2,1,0:T(8,128)S(1)}, f32[6,192,256]{2,1,0:T(8,128)S(1)}) custom-call(f32[12,192,256]{2,1,0:T(8,128)S(1)} %copy-done.1, f32[12,192,256]{2,1,0:T(8,128)S(1)} %copy-done.3, f32[1,12,192,256]{3,2,1,0:T(8,128)} %orb.9, f32[6,192,256]{2,1,0:T(8,128)S(1)} %shard_map.90.fo.uo, ...), custom_call_target="tpu_custom_call" | custom-call | tf_op jit(solution)/shard_map/pallas_call | solution.py:477
  50.6 2.3 %shard_map.94 = (f32[8,128]{1,0:T(8,128)S(1)}, f32[6,48,256]{2,1,0:T(8,128)}, f32[12,48,256]{2,1,0:T(8,128)}, f32[12,48,256]{2,1,0:T(8,128)}, f32[12,48,256]{2,1,0:T(8,128)}) custom-call(f32[6,192,256]{2,1,0:T(8,128)S(1)} %get-tuple-element.47.po, f32[6,192,256]{2,1,0:T(8,128)S(1)} %collective-permute-done.8.ho, f32[6,192,256]{2,1,0:T(8,128)S(1)} %get-tuple-element.52.to, ...), custom_call_target="tpu_custom_call" | custom-call | tf_op jit(solution)/shard_map/pallas_call | solution.py:486
  52.9 2.1 %collective-permute-start.13 = (f32[12,48,256]{2,1,0:T(8,128)}, f32[12,48,256]{2,1,0:T(8,128)S(1)}, u32[]{:S(2)}, u32[]{:S(2)}) collective-permute-start(f32[12,48,256]{2,1,0:T(8,128)} %get-tuple-element.67), channel_id=1, source_target_pairs={{0,64},{64,128},{128,192},{192,0},{1,65},{65,129},{129,193},{193,1... | collective-permute-start | bytes 1769480 | tf_op jit(solution)/shard_map/density_parts/ppermute | solution.py:405
  55.0 2.0 %collective-permute-start.14 = (f32[12,48,256]{2,1,0:T(8,128)}, f32[12,48,256]{2,1,0:T(8,128)S(1)}, u32[]{:S(2)}, u32[]{:S(2)}) collective-permute-start(f32[12,48,256]{2,1,0:T(8,128)} %get-tuple-element.68), channel_id=1, source_target_pairs={{0,128},{64,192},{128,0},{192,64},{1,129},{65,193},{129,1},{193,65... | collective-permute-start | bytes 1769480 | tf_op jit(solution)/shard_map/density_parts/ppermute | solution.py:405
  57.0 2.5 %collective-permute-start.15 = (f32[12,48,256]{2,1,0:T(8,128)}, f32[12,48,256]{2,1,0:T(8,128)}, u32[]{:S(2)}, u32[]{:S(2)}) collective-permute-start(f32[12,48,256]{2,1,0:T(8,128)} %get-tuple-element.69), channel_id=1, source_target_pairs={{0,192},{64,0},{128,64},{192,128},{1,193},{65,1},{129,65},{193,129... | collective-permute-start | bytes 1769480 | tf_op jit(solution)/shard_map/density_parts/ppermute | solution.py:405
  59.5 7.4 %collective-permute-start.12 = (f32[8,128]{1,0:T(8,128)S(1)}, f32[8,128]{1,0:T(8,128)S(1)}, u32[]{:S(2)}, u32[]{:S(2)}) collective-permute-start(f32[8,128]{1,0:T(8,128)S(1)} %get-tuple-element.62.row), channel_id=1, source_target_pairs={{0,1},{1,0},{2,3},{3,2},{4,5},{5,4},{6,7},{7,6},{8,9},{9,8},{10,11... | collective-permute-start | bytes 12296 | tf_op jit(solution)/shard_map/all_shares/ppermute | solution.py:499
  68.4 16.6 %all-to-all-start = ((f32[32,8,128]{2,1,0:T(8,128)}), f32[32,8,128]{2,1,0:T(8,128)}, u32[]{:S(2)}, u32[]{:S(2)}) async-start(f32[32,8,128]{2,1,0:T(8,128)} %all_shares.1), calls=%async_computation | async-start | bytes 262144 | tf_op jit(solution)/shard_map/all_shares/all_to_all | solution.py:500
  85.7 1.7 %shard_map.92.refs_0_.u = f32[12,192,256]{2,1,0:T(8,128)S(1)} custom-call(f32[12,192,256]{2,1,0:T(8,128)} %get-tuple-element.46.field), custom_call_target="tpu_custom_call" | custom-call | tf_op jit(solution)/shard_map/pallas_call | solution.py:501
  87.4 8.5 %all-to-all-done.shares = f32[32,8,128]{2,1,0:T(8,128)} async-done(((f32[32,8,128]{2,1,0:T(8,128)}), f32[32,8,128]{2,1,0:T(8,128)}, u32[]{:S(2)}, u32[]{:S(2)}) %all-to-all-start) | async-done | bytes 131104 | tf_op jit(solution)/shard_map/all_shares/all_to_all | solution.py:500
  95.8 1.9 %shard_map.95.coefs = f32[4,8,128]{2,1,0:T(8,128)} custom-call(f32[32,8,128]{2,1,0:T(8,128)} %all-to-all-done.shares, f32[1]{0:T(128)S(6)} %copy.10.freq, f32[12,192,256]{2,1,0:T(8,128)S(1)} %shard_map.92.refs_0_.u), custom_call_target="tpu_custom_call" | custom-call | tf_op jit(solution)/shard_map/pallas_call | solution.py:502
  97.7 4.5 %all-to-all-start.1 = ((f32[4,8,128]{2,1,0:T(8,128)}), f32[4,8,128]{2,1,0:T(8,128)S(1)}, u32[]{:S(2)}, u32[]{:S(2)}) async-start(f32[4,8,128]{2,1,0:T(8,128)} %shard_map.95.coefs), calls=%async_computation.1 | async-start | bytes 32768 | tf_op jit(solution)/shard_map/all_coefficients/all_to_all | solution.py:506
  102.3 3.4 %shard_map.96 = f32[1,12,192,256]{3,2,1,0:T(8,128)} custom-call(f32[12,192,256]{2,1,0:T(8,128)} %get-tuple-element.38.r, f32[12,192,256]{2,1,0:T(8,128)S(1)} %shard_map.92.refs_0_.u, f32[4,8,128]{2,1,0:T(8,128)} %shard_map.95.coefs), custom_call_target="tpu_custom_call" | custom-call | tf_op jit(solution)/shard_map/pallas_call | solution.py:507
  106.2 3.9 %shard_map.97 = f32[12,48,256]{2,1,0:T(8,128)} custom-call(f32[4,8,128]{2,1,0:T(8,128)S(1)} %all-to-all-done.1.coefs, f32[6,48,256]{2,1,0:T(8,128)} %get-tuple-element.63.refs_0_, f32[6,48,256]{2,1,0:T(8,128)} %copy-done.5, f32[6,48,256]{2,1,0:T(8,128)} %copy-done.6, f32[6,48,256]{2,1,0:T(8,128)} %copy-done.7, f32[6,48,256]{2,1,0:T(8,128)} %get-tuple-element.64.refs_4_, ...), custom_call_target="tpu_custom_call" | custom-call | tf_op jit(solution)/shard_map/pallas_call | solution.py:516
  (47 shorter events, 6.4 us)
Async XLA Ops:
  0.6 5.8 %copy-start.2 = (bf16[2,256,256]{2,1,0:T(8,128)(2,1)S(1)}, bf16[2,256,256]{2,1,0:T(8,128)(2,1)}, u32[]{:S(2)}) copy-start(bf16[2,256,256]{2,1,0:T(8,128)(2,1)} %constant.4.clone.mz) | copy-start | bytes 786436
  0.6 5.8 %copy-start.4 = (bf16[2,192,192]{2,1,0:T(8,128)(2,1)S(1)}, bf16[2,192,192]{2,1,0:T(8,128)(2,1)}, u32[]{:S(2)}) copy-start(bf16[2,192,192]{2,1,0:T(8,128)(2,1)} %constant.5.clone.my) | copy-start | bytes 442372
  0.7 5.7 %copy-start = (f32[12,192,256]{2,1,0:T(8,128)S(1)}, f32[12,192,256]{2,1,0:T(8,128)}, u32[]{:S(2)}) copy-start(f32[12,192,256]{2,1,0:T(8,128)} %pot.5) | copy-start | bytes 7077892
  3.5 2.9 %collective-permute-start = (f32[6,192,256]{2,1,0:T(8,128)S(1)}, f32[6,192,256]{2,1,0:T(8,128)S(1)}, u32[]{:S(2)}, u32[]{:S(2)}) collective-permute-start(f32[6,192,256]{2,1,0:T(8,128)S(1)} %get-tuple-element.37.fi), channel_id=1, source_target_pairs={{0,1},{1,0},{2,3},{3,2},{4,5},{5,4},{6,7},{7,6},{8,9},{9,8},{10,11... | collective-permute-start | bytes 3538952 | tf_op jit(solution)/shard_map/inner_swap/ppermute | solution.py:430
  3.6 11.0 %collective-permute-start.1 = (f32[6,192,256]{2,1,0:T(8,128)S(1)}, f32[6,192,256]{2,1,0:T(8,128)S(1)}, u32[]{:S(2)}, u32[]{:S(2)}) collective-permute-start(f32[6,192,256]{2,1,0:T(8,128)S(1)} %get-tuple-element.36.fo), channel_id=1, source_target_pairs={{1,2},{3,4},{5,6},{7,8},{9,10},{11,12},{13,14},{15,16},{17,18},{19... | collective-permute-start | bytes 3538952 | tf_op jit(solution)/shard_map/outer_swap/ppermute | solution.py:426
  13.1 7.6 %collective-permute-start.2 = (f32[6,192,256]{2,1,0:T(8,128)S(1)}, f32[6,192,256]{2,1,0:T(8,128)S(1)}, u32[]{:S(2)}, u32[]{:S(2)}) collective-permute-start(f32[6,192,256]{2,1,0:T(8,128)S(1)} %get-tuple-element.40.fi), channel_id=1, source_target_pairs={{0,1},{1,0},{2,3},{3,2},{4,5},{5,4},{6,7},{7,6},{8,9},{9,8},{10,11... | collective-permute-start | bytes 3538952 | tf_op jit(solution)/shard_map/inner_swap/ppermute | solution.py:430
  15.0 21.0 %collective-permute-start.3 = (f32[6,192,256]{2,1,0:T(8,128)S(1)}, f32[6,192,256]{2,1,0:T(8,128)S(1)}, u32[]{:S(2)}, u32[]{:S(2)}) collective-permute-start(f32[6,192,256]{2,1,0:T(8,128)S(1)} %shard_map.88.fo), channel_id=1, source_target_pairs={{1,2},{3,4},{5,6},{7,8},{9,10},{11,12},{13,14},{15,16},{17,18},{19... | collective-permute-start | bytes 3538952 | tf_op jit(solution)/shard_map/outer_swap/ppermute | solution.py:426
  15.8 20.2 %collective-permute-start.4 = (f32[6,48,256]{2,1,0:T(8,128)S(1)}, f32[6,48,256]{2,1,0:T(8,128)S(1)}, u32[]{:S(2)}, u32[]{:S(2)}) collective-permute-start(f32[6,48,256]{2,1,0:T(8,128)S(1)} %get-tuple-element.42), channel_id=1, source_target_pairs={{0,64},{64,128},{128,192},{192,0},{1,65},{65,129},{129,193},{193,1... | collective-permute-start | bytes 884744 | tf_op jit(solution)/shard_map/density_parts/ppermute | solution.py:405
  17.4 18.6 %collective-permute-start.5 = (f32[6,48,256]{2,1,0:T(8,128)S(1)}, f32[6,48,256]{2,1,0:T(8,128)S(1)}, u32[]{:S(2)}, u32[]{:S(2)}) collective-permute-start(f32[6,48,256]{2,1,0:T(8,128)S(1)} %get-tuple-element.43), channel_id=1, source_target_pairs={{0,128},{64,192},{128,0},{192,64},{1,129},{65,193},{129,1},{193,65... | collective-permute-start | bytes 884744 | tf_op jit(solution)/shard_map/density_parts/ppermute | solution.py:405
  19.0 17.0 %collective-permute-start.6 = (f32[6,48,256]{2,1,0:T(8,128)S(1)}, f32[6,48,256]{2,1,0:T(8,128)S(1)}, u32[]{:S(2)}, u32[]{:S(2)}) collective-permute-start(f32[6,48,256]{2,1,0:T(8,128)S(1)} %get-tuple-element.44), channel_id=1, source_target_pairs={{0,192},{64,0},{128,64},{192,128},{1,193},{65,1},{129,65},{193,129... | collective-permute-start | bytes 884744 | tf_op jit(solution)/shard_map/density_parts/ppermute | solution.py:405
  27.5 13.1 %collective-permute-start.7 = (f32[6,192,256]{2,1,0:T(8,128)S(1)}, f32[6,192,256]{2,1,0:T(8,128)S(1)}, u32[]{:S(2)}, u32[]{:S(2)}) collective-permute-start(f32[6,192,256]{2,1,0:T(8,128)S(1)} %get-tuple-element.45.fi.ui), channel_id=1, source_target_pairs={{0,1},{1,0},{2,3},{3,2},{4,5},{5,4},{6,7},{7,6},{8,9},{9,8},{10,11... | collective-permute-start | bytes 3538952 | tf_op jit(solution)/shard_map/inner_swap/ppermute | solution.py:430
  37.0 13.6 %collective-permute-start.8 = (f32[6,192,256]{2,1,0:T(8,128)S(1)}, f32[6,192,256]{2,1,0:T(8,128)S(1)}, u32[]{:S(2)}, u32[]{:S(2)}) collective-permute-start(f32[6,192,256]{2,1,0:T(8,128)S(1)} %shard_map.90.fo.uo), channel_id=1, source_target_pairs={{1,2},{3,4},{5,6},{7,8},{9,10},{11,12},{13,14},{15,16},{17,18},{19... | collective-permute-start | bytes 3538952 | tf_op jit(solution)/shard_map/outer_swap/ppermute | solution.py:426
  37.7 12.8 %collective-permute-start.10 = (f32[6,48,256]{2,1,0:T(8,128)S(1)}, f32[6,48,256]{2,1,0:T(8,128)S(1)}, u32[]{:S(2)}, u32[]{:S(2)}) collective-permute-start(f32[6,48,256]{2,1,0:T(8,128)S(1)} %get-tuple-element.60), channel_id=1, source_target_pairs={{0,128},{64,192},{128,0},{192,64},{1,129},{65,193},{129,1},{193,65... | collective-permute-start | bytes 884744 | tf_op jit(solution)/shard_map/density_parts/ppermute | solution.py:405
  38.2 12.3 %collective-permute-start.11 = (f32[6,48,256]{2,1,0:T(8,128)S(1)}, f32[6,48,256]{2,1,0:T(8,128)S(1)}, u32[]{:S(2)}, u32[]{:S(2)}) collective-permute-start(f32[6,48,256]{2,1,0:T(8,128)S(1)} %get-tuple-element.61), channel_id=1, source_target_pairs={{0,192},{64,0},{128,64},{192,128},{1,193},{65,1},{129,65},{193,129... | collective-permute-start | bytes 884744 | tf_op jit(solution)/shard_map/density_parts/ppermute | solution.py:405
  40.4 10.1 %collective-permute-start.9 = (f32[6,48,256]{2,1,0:T(8,128)S(1)}, f32[6,48,256]{2,1,0:T(8,128)S(1)}, u32[]{:S(2)}, u32[]{:S(2)}) collective-permute-start(f32[6,48,256]{2,1,0:T(8,128)S(1)} %get-tuple-element.59), channel_id=1, source_target_pairs={{0,64},{64,128},{128,192},{192,0},{1,65},{65,129},{129,193},{193,1... | collective-permute-start | bytes 884744 | tf_op jit(solution)/shard_map/density_parts/ppermute | solution.py:405
  40.6 7.2 %copy-start.1 = (f32[12,192,256]{2,1,0:T(8,128)S(1)}, f32[12,192,256]{2,1,0:T(8,128)}, u32[]{:S(2)}) copy-start(f32[12,192,256]{2,1,0:T(8,128)} %get-tuple-element.38.r) | copy-start | bytes 7077892
  40.6 7.2 %copy-start.3 = (f32[12,192,256]{2,1,0:T(8,128)S(1)}, f32[12,192,256]{2,1,0:T(8,128)}, u32[]{:S(2)}) copy-start(f32[12,192,256]{2,1,0:T(8,128)} %get-tuple-element.48.t_kept) | copy-start | bytes 7077892
  50.5 2.3 %copy-start.8 = (f32[6,48,256]{2,1,0:T(8,128)}, f32[6,48,256]{2,1,0:T(8,128)S(1)}, u32[]{:S(2)}) copy-start(f32[6,48,256]{2,1,0:T(8,128)S(1)} %collective-permute-done.10.refs_4_.refs_6_) | copy-start | bytes 884740
  52.9 53.3 %collective-permute-start.13 = (f32[12,48,256]{2,1,0:T(8,128)}, f32[12,48,256]{2,1,0:T(8,128)S(1)}, u32[]{:S(2)}, u32[]{:S(2)}) collective-permute-start(f32[12,48,256]{2,1,0:T(8,128)} %get-tuple-element.67), channel_id=1, source_target_pairs={{0,64},{64,128},{128,192},{192,0},{1,65},{65,129},{129,193},{193,1... | collective-permute-start | bytes 1769480 | tf_op jit(solution)/shard_map/density_parts/ppermute | solution.py:405
  55.0 51.2 %collective-permute-start.14 = (f32[12,48,256]{2,1,0:T(8,128)}, f32[12,48,256]{2,1,0:T(8,128)S(1)}, u32[]{:S(2)}, u32[]{:S(2)}) collective-permute-start(f32[12,48,256]{2,1,0:T(8,128)} %get-tuple-element.68), channel_id=1, source_target_pairs={{0,128},{64,192},{128,0},{192,64},{1,129},{65,193},{129,1},{193,65... | collective-permute-start | bytes 1769480 | tf_op jit(solution)/shard_map/density_parts/ppermute | solution.py:405
  57.0 49.2 %collective-permute-start.15 = (f32[12,48,256]{2,1,0:T(8,128)}, f32[12,48,256]{2,1,0:T(8,128)}, u32[]{:S(2)}, u32[]{:S(2)}) collective-permute-start(f32[12,48,256]{2,1,0:T(8,128)} %get-tuple-element.69), channel_id=1, source_target_pairs={{0,192},{64,0},{128,64},{192,128},{1,193},{65,1},{129,65},{193,129... | collective-permute-start | bytes 1769480 | tf_op jit(solution)/shard_map/density_parts/ppermute | solution.py:405
  59.5 8.2 %collective-permute-start.12 = (f32[8,128]{1,0:T(8,128)S(1)}, f32[8,128]{1,0:T(8,128)S(1)}, u32[]{:S(2)}, u32[]{:S(2)}) collective-permute-start(f32[8,128]{1,0:T(8,128)S(1)} %get-tuple-element.62.row), channel_id=1, source_target_pairs={{0,1},{1,0},{2,3},{3,2},{4,5},{5,4},{6,7},{7,6},{8,9},{9,8},{10,11... | collective-permute-start | bytes 12296 | tf_op jit(solution)/shard_map/all_shares/ppermute | solution.py:499
  68.4 27.4 %all-to-all-start = ((f32[32,8,128]{2,1,0:T(8,128)}), f32[32,8,128]{2,1,0:T(8,128)}, u32[]{:S(2)}, u32[]{:S(2)}) async-start(f32[32,8,128]{2,1,0:T(8,128)} %all_shares.1), calls=%async_computation | async-start | bytes 262144 | tf_op jit(solution)/shard_map/all_shares/all_to_all | solution.py:500
  97.7 8.5 %all-to-all-start.1 = ((f32[4,8,128]{2,1,0:T(8,128)}), f32[4,8,128]{2,1,0:T(8,128)S(1)}, u32[]{:S(2)}, u32[]{:S(2)}) async-start(f32[4,8,128]{2,1,0:T(8,128)} %shard_map.95.coefs), calls=%async_computation.1 | async-start | bytes 32768 | tf_op jit(solution)/shard_map/all_coefficients/all_to_all | solution.py:506
  (5 other events, 7.1 us)

commit v3 on v2

--- a/solution.py
+++ b/solution.py
@@ -302,14 +302,7 @@
         out[i] = both
 
 
-def preload_kernel(field, out, sem):
-    load = pltpu.make_async_copy(field, out, sem.at[0])
-    load.start()
-    load.wait()
-
-
-def coefficient_kernel(shares, freq, *refs):
-    out = refs[-1]
+def coefficient_kernel(shares, freq, out):
     w2 = freq[0] * freq[0]
     share = jnp.concatenate([shares[:, 0, :], shares[:, 1, :]], axis=0)
     rr, tt, s0, s1, own, t0, t1 = (share[:, i : i + 1] for i in range(7))
@@ -337,24 +330,29 @@
     return tuple(broad(one[4 * i : 4 * i + 1, 0:1], shape) for i in range(2))
 
 
-def solution_kernel(r, u, coefs, sol, rbuf, xbuf, in_sems, out_sems):
+def solution_kernel(r, u, coefs, sol, rbuf, ubuf, xbuf, in_sems, out_sems):
     core = core_index()
 
-    def field(m):
-        return pltpu.make_async_copy(r.at[m], rbuf.at[m], in_sems.at[m])
+    def fields(m):
+        return (
+            pltpu.make_async_copy(r.at[m], rbuf.at[m], in_sems.at[0, m]),
+            pltpu.make_async_copy(u.at[m], ubuf.at[m], in_sems.at[1, m]),
+        )
 
     def store(m):
         return pltpu.make_async_copy(xbuf.at[m], sol.at[0, plane_of(m, core)], out_sems.at[m])
 
     for m in range(2 * W):
-        field(m).start()
+        for c in fields(m):
+            c.start()
     p, q = both_of(coefs, 0, (8, r.shape[2]))
     for m in range(2 * W):
-        field(m).wait()
+        for c in fields(m):
+            c.wait()
 
         def row(t, _, m=m):
             rows = rows_of(t)
-            xbuf[m, rows, :] = p * rbuf[m, rows, :] + q * u[m, rows, :]
+            xbuf[m, rows, :] = p * rbuf[m, rows, :] + q * ubuf[m, rows, :]
             return 0
 
         lax.fori_loop(0, r.shape[1] // 8, row, 0, unroll=8)
@@ -498,20 +496,19 @@
             copies_kernel, jax.ShapeDtypeStruct((ngrid // 2, 8, 128), F32), [VM, VM], VM, limit=4
         )(shares, lax.ppermute(shares, GRID, inner_pairs))
         shares = lax.all_to_all(shares, "chip", 0, 0, tiled=True)
-    u_all = call(preload_kernel, whole, [ANY], VM, [pltpu.SemaphoreType.DMA((1,))], limit=4)(in_hbm(u_kept))
-    coefs = call(coefficient_kernel, jax.ShapeDtypeStruct((norb, 8, 128), F32), [VM, SM, VM], VM, limit=4)(
-        shares, frequency, u_all
+    coefs = call(coefficient_kernel, jax.ShapeDtypeStruct((norb, 8, 128), F32), [VM, SM], VM, limit=4)(
+        shares, frequency
     )
     with jax.named_scope("all_coefficients"):
         all_coefs = lax.all_to_all(coefs, "orb", 0, 0, tiled=True)
     solution = call(
         solution_kernel,
         in_hbm_type(jax.ShapeDtypeStruct((1, nx, ny, nz), F32)),
-        [ANY, VM, VM],
+        [ANY, ANY, VM],
         ANY,
-        [pltpu.VMEM(whole.shape, F32)] * 2 + [pltpu.SemaphoreType.DMA((nx,))] * 2,
+        [pltpu.VMEM(whole.shape, F32)] * 3 + [pltpu.SemaphoreType.DMA((2, nx)), pltpu.SemaphoreType.DMA((nx,))],
         limit=9,
-    )(in_hbm(r_kept), u_all, coefs)
+    )(in_hbm(r_kept), in_hbm(u_kept), coefs)
     waiting = [in_hbm(x) for x in (*parts_ti, *parts_to, own_vo, parts[0])]
     density = call(
         functools.partial(density_kernel, count=norb),

time: 111 us -> 109 us (0.982)
  Pallas kernels: 40.7 us -> 38.4 us
  waiting for transfers between devices: 11.2 us -> 12.5 us
    all_to_all x1, waiting for transfers between devices: 8.46 us -> 10.2 us  [body(): shares = lax.all_to_all(shares, 'chip', 0, 0, tiled=True)]
    pallas_call x1 -> x0, Pallas kernels: 1.67 us -> none  [body(): call(preload_kernel, whole, [ANY], VM, [pltpu.SemaphoreType.DMA((1,))], l...]
    pallas_call x1, Pallas kernels: 3.42 us -> 4.76 us  [body(): call(solution_kernel, in_hbm_type(jax.ShapeDtypeStruct((1, nx, ny, nz), F...]
  transfers between devices with their start and end apart: 18 -> 18, of which waited for: 4 -> 3; matrix products, arithmetic and copies ran while one was open for 0% -> 0% of each run, Pallas kernels for 29% -> 28%
where the time goes in v3:
time: 109 us
  starting transfers between devices  55.4 us (51%)
  Pallas kernels  38.4 us (35%)
  waiting for transfers between devices  12.5 us (11%)
  between operations  2.24 us (2%)
    pallas_call x3, Pallas kernels, local(): call(functools.partial(local_kernel, stage=stage, count=norb), (half, hal...  20.5 us
    all_to_all x1, starting transfers between devices, body(): shares = lax.all_to_all(shares, 'chip', 0, 0, tiled=True)  16.6 us
    ppermute x9, starting transfers between devices, shift(): lax.ppermute(value, axis, [(i, (i + d) % count) for i in range(count)])  14.6 us
    all_to_all x1, waiting for transfers between devices, body(): shares = lax.all_to_all(shares, 'chip', 0, 0, tiled=True)  10.2 us
    ppermute x3, starting transfers between devices, inner_swap(): return in_vmem(lax.ppermute(x, GRID, inner_pairs))  10.1 us
    ppermute x1, starting transfers between devices, body(): lax.ppermute(shares, GRID, inner_pairs)  7.36 us
    pallas_call x1, Pallas kernels, body(): call(solution_kernel, in_hbm_type(jax.ShapeDtypeStruct((1, nx, ny, nz), F...  4.76 us
    all_to_all x1, starting transfers between devices, body(): all_coefs = lax.all_to_all(coefs, 'orb', 0, 0, tiled=True)  4.55 us
  transfers between devices with their start and end apart: 18, of which 3 were waited for; matrix products, arithmetic and copies ran while one was open for 0% of the time, Pallas kernels for 28%

profile of v3, /device:TPU:8, one launch (start us, length us, event | category | flops | bytes accessed | tf_op | source)
XLA Modules:
  0.0 109.0 jit_solution(10925209078084301480)
XLA Ops:
  0.7 2.8 %shard_map.86 = (f32[6,192,256]{2,1,0:T(8,128)S(1)}, f32[6,192,256]{2,1,0:T(8,128)S(1)}) custom-call(f32[1,12,192,256]{3,2,1,0:T(8,128)} %orb.9, f32[12,192,256]{2,1,0:T(8,128)} %trial.1), custom_call_target="tpu_custom_call" | custom-call | tf_op jit(solution)/shard_map/pallas_call | solution.py:455
  4.9 1.4 %collective-permute-done.hi_halo = f32[6,192,256]{2,1,0:T(8,128)S(1)} collective-permute-done((f32[6,192,256]{2,1,0:T(8,128)S(1)}, f32[6,192,256]{2,1,0:T(8,128)S(1)}, u32[]{:S(2)}, u32[]{:S(2)}) %collective-permute-start) | collective-permute-done | bytes 1179680 | tf_op jit(solution)/shard_map/inner_swap/ppermute | solution.py:428
  6.4 6.7 %shard_map.87 = (f32[6,192,256]{2,1,0:T(8,128)S(1)}, f32[6,192,256]{2,1,0:T(8,128)S(1)}, f32[8,128]{1,0:T(8,128)S(1)}, f32[6,48,256]{2,1,0:T(8,128)}, f32[12,192...) custom-call(f32[6,192,256]{2,1,0:T(8,128)S(1)} %get-tuple-element.36.fo, ...), custom_call_target="tpu_custom_call" | custom-call | tf_op jit(solution)/shard_map/pallas_call | solution.py:432
  13.1 1.5 %collective-permute-start.2 = (f32[6,192,256]{2,1,0:T(8,128)S(1)}, f32[6,192,256]{2,1,0:T(8,128)S(1)}, u32[]{:S(2)}, u32[]{:S(2)}) collective-permute-start(f32[6,192,256]{2,1,0:T(8,128)S(1)} %get-tuple-element.40.fi), channel_id=1, source_target_pairs={{0,1},{1,0},{2,3},{3,2},{4,5},{5,4},{6,7},{7,6},{8,9},{9,8},{10,11... | collective-permute-start | bytes 3538952 | tf_op jit(solution)/shard_map/inner_swap/ppermute | solution.py:428
  15.7 1.7 %collective-permute-start.4 = (f32[6,48,256]{2,1,0:T(8,128)S(1)}, f32[6,48,256]{2,1,0:T(8,128)S(1)}, u32[]{:S(2)}, u32[]{:S(2)}) collective-permute-start(f32[6,48,256]{2,1,0:T(8,128)S(1)} %get-tuple-element.42), channel_id=1, source_target_pairs={{0,64},{64,128},{128,192},{192,0},{1,65},{65,129},{129,193},{193,1... | collective-permute-start | bytes 884744 | tf_op jit(solution)/shard_map/density_parts/ppermute | solution.py:403
  17.4 1.6 %collective-permute-start.5 = (f32[6,48,256]{2,1,0:T(8,128)S(1)}, f32[6,48,256]{2,1,0:T(8,128)S(1)}, u32[]{:S(2)}, u32[]{:S(2)}) collective-permute-start(f32[6,48,256]{2,1,0:T(8,128)S(1)} %get-tuple-element.43), channel_id=1, source_target_pairs={{0,128},{64,192},{128,0},{192,64},{1,129},{65,193},{129,1},{193,65... | collective-permute-start | bytes 884744 | tf_op jit(solution)/shard_map/density_parts/ppermute | solution.py:403
  19.0 1.8 %collective-permute-start.6 = (f32[6,48,256]{2,1,0:T(8,128)S(1)}, f32[6,48,256]{2,1,0:T(8,128)S(1)}, u32[]{:S(2)}, u32[]{:S(2)}) collective-permute-start(f32[6,48,256]{2,1,0:T(8,128)S(1)} %get-tuple-element.44), channel_id=1, source_target_pairs={{0,192},{64,0},{128,64},{192,128},{1,193},{65,1},{129,65},{193,129... | collective-permute-start | bytes 884744 | tf_op jit(solution)/shard_map/density_parts/ppermute | solution.py:403
  20.7 6.7 %shard_map.89 = (f32[6,192,256]{2,1,0:T(8,128)S(1)}, f32[6,192,256]{2,1,0:T(8,128)S(1)}, f32[8,128]{1,0:T(8,128)S(1)}, f32[6,48,256]{2,1,0:T(8,128)}, f32[12,192...) custom-call(f32[6,192,256]{2,1,0:T(8,128)S(1)} %shard_map.88.fo, ...), custom_call_target="tpu_custom_call" | custom-call | tf_op jit(solution)/shard_map/pallas_call | solution.py:432
  27.5 8.5 %collective-permute-start.7 = (f32[6,192,256]{2,1,0:T(8,128)S(1)}, f32[6,192,256]{2,1,0:T(8,128)S(1)}, u32[]{:S(2)}, u32[]{:S(2)}) collective-permute-start(f32[6,192,256]{2,1,0:T(8,128)S(1)} %get-tuple-element.45.fi.ui), channel_id=1, source_target_pairs={{0,1},{1,0},{2,3},{3,2},{4,5},{5,4},{6,7},{7,6},{8,9},{9,8},{10,11... | collective-permute-start | bytes 3538952 | tf_op jit(solution)/shard_map/inner_swap/ppermute | solution.py:428
  38.2 2.1 %collective-permute-start.11 = (f32[6,48,256]{2,1,0:T(8,128)S(1)}, f32[6,48,256]{2,1,0:T(8,128)S(1)}, u32[]{:S(2)}, u32[]{:S(2)}) collective-permute-start(f32[6,48,256]{2,1,0:T(8,128)S(1)} %get-tuple-element.61), channel_id=1, source_target_pairs={{0,192},{64,0},{128,64},{192,128},{1,193},{65,1},{129,65},{193,129... | collective-permute-start | bytes 884744 | tf_op jit(solution)/shard_map/density_parts/ppermute | solution.py:403
  40.6 7.1 %shard_map.91 = (f32[6,192,256]{2,1,0:T(8,128)S(1)}, f32[6,192,256]{2,1,0:T(8,128)S(1)}, f32[8,128]{1,0:T(8,128)}, f32[6,48,256]{2,1,0:T(8,128)}, f32[12,192,256...) custom-call(f32[6,192,256]{2,1,0:T(8,128)S(1)} %shard_map.90.fo.uo, ...), custom_call_target="tpu_custom_call" | custom-call | tf_op jit(solution)/shard_map/pallas_call | solution.py:432
  47.7 2.7 %shard_map.92 = (f32[8,128]{1,0:T(8,128)S(1)}, f32[2,8,128]{2,1,0:T(8,128)S(1)}, f32[6,192,256]{2,1,0:T(8,128)S(1)}, f32[6,192,256]{2,1,0:T(8,128)S(1)}) custom-call(f32[12,192,256]{2,1,0:T(8,128)S(1)} %copy-done.1, f32[12,192,256]{2,1,0:T(8,128)S(1)} %copy-done.3, f32[1,12,192,256]{3,2,1,0:T(8,128)} %orb.9, f32[6,192,256]{2,1,0:T(8,128)S(1)} %shard_map.90.fo.uo, ...), custom_call_target="tpu_custom_call" | custom-call | tf_op jit(solution)/shard_map/pallas_call | solution.py:475
  50.5 2.3 %shard_map.93 = (f32[8,128]{1,0:T(8,128)S(1)}, f32[6,48,256]{2,1,0:T(8,128)}, f32[12,48,256]{2,1,0:T(8,128)}, f32[12,48,256]{2,1,0:T(8,128)}, f32[12,48,256]{2,1,0:T(8,128)}) custom-call(f32[6,192,256]{2,1,0:T(8,128)S(1)} %get-tuple-element.47.po, f32[6,192,256]{2,1,0:T(8,128)S(1)} %collective-permute-done.8.ho, f32[6,192,256]{2,1,0:T(8,128)S(1)} %get-tuple-element.52.to, ...), custom_call_target="tpu_custom_call" | custom-call | tf_op jit(solution)/shard_map/pallas_call | solution.py:484
  52.8 2.1 %collective-permute-start.13 = (f32[12,48,256]{2,1,0:T(8,128)}, f32[12,48,256]{2,1,0:T(8,128)S(1)}, u32[]{:S(2)}, u32[]{:S(2)}) collective-permute-start(f32[12,48,256]{2,1,0:T(8,128)} %get-tuple-element.67), channel_id=1, source_target_pairs={{0,64},{64,128},{128,192},{192,0},{1,65},{65,129},{129,193},{193,1... | collective-permute-start | bytes 1769480 | tf_op jit(solution)/shard_map/density_parts/ppermute | solution.py:403
  54.9 2.0 %collective-permute-start.14 = (f32[12,48,256]{2,1,0:T(8,128)}, f32[12,48,256]{2,1,0:T(8,128)S(1)}, u32[]{:S(2)}, u32[]{:S(2)}) collective-permute-start(f32[12,48,256]{2,1,0:T(8,128)} %get-tuple-element.68), channel_id=1, source_target_pairs={{0,128},{64,192},{128,0},{192,64},{1,129},{65,193},{129,1},{193,65... | collective-permute-start | bytes 1769480 | tf_op jit(solution)/shard_map/density_parts/ppermute | solution.py:403
  56.9 2.5 %collective-permute-start.15 = (f32[12,48,256]{2,1,0:T(8,128)}, f32[12,48,256]{2,1,0:T(8,128)S(1)}, u32[]{:S(2)}, u32[]{:S(2)}) collective-permute-start(f32[12,48,256]{2,1,0:T(8,128)} %get-tuple-element.69), channel_id=1, source_target_pairs={{0,192},{64,0},{128,64},{192,128},{1,193},{65,1},{129,65},{193,129... | collective-permute-start | bytes 1769480 | tf_op jit(solution)/shard_map/density_parts/ppermute | solution.py:403
  59.4 7.4 %collective-permute-start.12 = (f32[8,128]{1,0:T(8,128)S(1)}, f32[8,128]{1,0:T(8,128)S(1)}, u32[]{:S(2)}, u32[]{:S(2)}) collective-permute-start(f32[8,128]{1,0:T(8,128)S(1)} %get-tuple-element.62.row), channel_id=1, source_target_pairs={{0,1},{1,0},{2,3},{3,2},{4,5},{5,4},{6,7},{7,6},{8,9},{9,8},{10,11... | collective-permute-start | bytes 12296 | tf_op jit(solution)/shard_map/all_shares/ppermute | solution.py:497
  66.8 0.8 collective-permute-done.12.other
  68.3 16.6 %all-to-all-start = ((f32[32,8,128]{2,1,0:T(8,128)}), f32[32,8,128]{2,1,0:T(8,128)S(1)}, u32[]{:S(2)}, u32[]{:S(2)}) async-start(f32[32,8,128]{2,1,0:T(8,128)} %all_shares.1), calls=%async_computation | async-start | bytes 262144 | tf_op jit(solution)/shard_map/all_shares/all_to_all | solution.py:498
  85.6 10.2 %all-to-all-done.shares = f32[32,8,128]{2,1,0:T(8,128)S(1)} async-done(((f32[32,8,128]{2,1,0:T(8,128)}), f32[32,8,128]{2,1,0:T(8,128)S(1)}, u32[]{:S(2)}, u32[]{:S(2)}) %all-to-all-start) | async-done | bytes 131104 | tf_op jit(solution)/shard_map/all_shares/all_to_all | solution.py:498
  95.7 1.0 shard_map.94.coefs
  96.7 4.6 %all-to-all-start.1 = ((f32[4,8,128]{2,1,0:T(8,128)}), f32[4,8,128]{2,1,0:T(8,128)S(1)}, u32[]{:S(2)}, u32[]{:S(2)}) async-start(f32[4,8,128]{2,1,0:T(8,128)} %shard_map.94.coefs), calls=%async_computation.1 | async-start | bytes 32768 | tf_op jit(solution)/shard_map/all_coefficients/all_to_all | solution.py:503
  101.3 4.8 %shard_map.95 = f32[1,12,192,256]{3,2,1,0:T(8,128)} custom-call(f32[12,192,256]{2,1,0:T(8,128)} %get-tuple-element.38.r, f32[12,192,256]{2,1,0:T(8,128)} %get-tuple-element.46.u, f32[4,8,128]{2,1,0:T(8,128)} %shard_map.94.coefs), custom_call_target="tpu_custom_call" | custom-call | tf_op jit(solution)/shard_map/pallas_call | solution.py:504
  106.1 2.9 %shard_map.96 = f32[12,48,256]{2,1,0:T(8,128)} custom-call(f32[4,8,128]{2,1,0:T(8,128)S(1)} %all-to-all-done.1.coefs, f32[6,48,256]{2,1,0:T(8,128)} %get-tuple-element.63.refs_0_, f32[6,48,256]{2,1,0:T(8,128)} %copy-done.5, f32[6,48,256]{2,1,0:T(8,128)} %copy-done.6, f32[6,48,256]{2,1,0:T(8,128)} %copy-done.7, f32[6,48,256]{2,1,0:T(8,128)} %get-tuple-element.64.refs_4_, ...), custom_call_target="tpu_custom_call" | custom-call | tf_op jit(solution)/shard_map/pallas_call | solution.py:513
  (46 shorter events, 5.1 us)
Async XLA Ops:
  0.6 5.8 %copy-start.2 = (bf16[2,256,256]{2,1,0:T(8,128)(2,1)S(1)}, bf16[2,256,256]{2,1,0:T(8,128)(2,1)}, u32[]{:S(2)}) copy-start(bf16[2,256,256]{2,1,0:T(8,128)(2,1)} %constant.4.clone.mz) | copy-start | bytes 786436
  0.6 5.8 %copy-start.4 = (bf16[2,192,192]{2,1,0:T(8,128)(2,1)S(1)}, bf16[2,192,192]{2,1,0:T(8,128)(2,1)}, u32[]{:S(2)}) copy-start(bf16[2,192,192]{2,1,0:T(8,128)(2,1)} %constant.5.clone.my) | copy-start | bytes 442372
  0.7 5.7 %copy-start = (f32[12,192,256]{2,1,0:T(8,128)S(1)}, f32[12,192,256]{2,1,0:T(8,128)}, u32[]{:S(2)}) copy-start(f32[12,192,256]{2,1,0:T(8,128)} %pot.5) | copy-start | bytes 7077892
  3.5 2.9 %collective-permute-start = (f32[6,192,256]{2,1,0:T(8,128)S(1)}, f32[6,192,256]{2,1,0:T(8,128)S(1)}, u32[]{:S(2)}, u32[]{:S(2)}) collective-permute-start(f32[6,192,256]{2,1,0:T(8,128)S(1)} %get-tuple-element.37.fi), channel_id=1, source_target_pairs={{0,1},{1,0},{2,3},{3,2},{4,5},{5,4},{6,7},{7,6},{8,9},{9,8},{10,11... | collective-permute-start | bytes 3538952 | tf_op jit(solution)/shard_map/inner_swap/ppermute | solution.py:428
  3.6 11.0 %collective-permute-start.1 = (f32[6,192,256]{2,1,0:T(8,128)S(1)}, f32[6,192,256]{2,1,0:T(8,128)S(1)}, u32[]{:S(2)}, u32[]{:S(2)}) collective-permute-start(f32[6,192,256]{2,1,0:T(8,128)S(1)} %get-tuple-element.36.fo), channel_id=1, source_target_pairs={{1,2},{3,4},{5,6},{7,8},{9,10},{11,12},{13,14},{15,16},{17,18},{19... | collective-permute-start | bytes 3538952 | tf_op jit(solution)/shard_map/outer_swap/ppermute | solution.py:424
  13.1 7.6 %collective-permute-start.2 = (f32[6,192,256]{2,1,0:T(8,128)S(1)}, f32[6,192,256]{2,1,0:T(8,128)S(1)}, u32[]{:S(2)}, u32[]{:S(2)}) collective-permute-start(f32[6,192,256]{2,1,0:T(8,128)S(1)} %get-tuple-element.40.fi), channel_id=1, source_target_pairs={{0,1},{1,0},{2,3},{3,2},{4,5},{5,4},{6,7},{7,6},{8,9},{9,8},{10,11... | collective-permute-start | bytes 3538952 | tf_op jit(solution)/shard_map/inner_swap/ppermute | solution.py:428
  15.0 21.0 %collective-permute-start.3 = (f32[6,192,256]{2,1,0:T(8,128)S(1)}, f32[6,192,256]{2,1,0:T(8,128)S(1)}, u32[]{:S(2)}, u32[]{:S(2)}) collective-permute-start(f32[6,192,256]{2,1,0:T(8,128)S(1)} %shard_map.88.fo), channel_id=1, source_target_pairs={{1,2},{3,4},{5,6},{7,8},{9,10},{11,12},{13,14},{15,16},{17,18},{19... | collective-permute-start | bytes 3538952 | tf_op jit(solution)/shard_map/outer_swap/ppermute | solution.py:424
  15.7 20.3 %collective-permute-start.4 = (f32[6,48,256]{2,1,0:T(8,128)S(1)}, f32[6,48,256]{2,1,0:T(8,128)S(1)}, u32[]{:S(2)}, u32[]{:S(2)}) collective-permute-start(f32[6,48,256]{2,1,0:T(8,128)S(1)} %get-tuple-element.42), channel_id=1, source_target_pairs={{0,64},{64,128},{128,192},{192,0},{1,65},{65,129},{129,193},{193,1... | collective-permute-start | bytes 884744 | tf_op jit(solution)/shard_map/density_parts/ppermute | solution.py:403
  17.4 18.6 %collective-permute-start.5 = (f32[6,48,256]{2,1,0:T(8,128)S(1)}, f32[6,48,256]{2,1,0:T(8,128)S(1)}, u32[]{:S(2)}, u32[]{:S(2)}) collective-permute-start(f32[6,48,256]{2,1,0:T(8,128)S(1)} %get-tuple-element.43), channel_id=1, source_target_pairs={{0,128},{64,192},{128,0},{192,64},{1,129},{65,193},{129,1},{193,65... | collective-permute-start | bytes 884744 | tf_op jit(solution)/shard_map/density_parts/ppermute | solution.py:403
  19.0 17.1 %collective-permute-start.6 = (f32[6,48,256]{2,1,0:T(8,128)S(1)}, f32[6,48,256]{2,1,0:T(8,128)S(1)}, u32[]{:S(2)}, u32[]{:S(2)}) collective-permute-start(f32[6,48,256]{2,1,0:T(8,128)S(1)} %get-tuple-element.44), channel_id=1, source_target_pairs={{0,192},{64,0},{128,64},{192,128},{1,193},{65,1},{129,65},{193,129... | collective-permute-start | bytes 884744 | tf_op jit(solution)/shard_map/density_parts/ppermute | solution.py:403
  27.5 13.1 %collective-permute-start.7 = (f32[6,192,256]{2,1,0:T(8,128)S(1)}, f32[6,192,256]{2,1,0:T(8,128)S(1)}, u32[]{:S(2)}, u32[]{:S(2)}) collective-permute-start(f32[6,192,256]{2,1,0:T(8,128)S(1)} %get-tuple-element.45.fi.ui), channel_id=1, source_target_pairs={{0,1},{1,0},{2,3},{3,2},{4,5},{5,4},{6,7},{7,6},{8,9},{9,8},{10,11... | collective-permute-start | bytes 3538952 | tf_op jit(solution)/shard_map/inner_swap/ppermute | solution.py:428
  36.9 13.5 %collective-permute-start.8 = (f32[6,192,256]{2,1,0:T(8,128)S(1)}, f32[6,192,256]{2,1,0:T(8,128)S(1)}, u32[]{:S(2)}, u32[]{:S(2)}) collective-permute-start(f32[6,192,256]{2,1,0:T(8,128)S(1)} %shard_map.90.fo.uo), channel_id=1, source_target_pairs={{1,2},{3,4},{5,6},{7,8},{9,10},{11,12},{13,14},{15,16},{17,18},{19... | collective-permute-start | bytes 3538952 | tf_op jit(solution)/shard_map/outer_swap/ppermute | solution.py:424
  37.7 12.8 %collective-permute-start.10 = (f32[6,48,256]{2,1,0:T(8,128)S(1)}, f32[6,48,256]{2,1,0:T(8,128)S(1)}, u32[]{:S(2)}, u32[]{:S(2)}) collective-permute-start(f32[6,48,256]{2,1,0:T(8,128)S(1)} %get-tuple-element.60), channel_id=1, source_target_pairs={{0,128},{64,192},{128,0},{192,64},{1,129},{65,193},{129,1},{193,65... | collective-permute-start | bytes 884744 | tf_op jit(solution)/shard_map/density_parts/ppermute | solution.py:403
  38.2 12.2 %collective-permute-start.11 = (f32[6,48,256]{2,1,0:T(8,128)S(1)}, f32[6,48,256]{2,1,0:T(8,128)S(1)}, u32[]{:S(2)}, u32[]{:S(2)}) collective-permute-start(f32[6,48,256]{2,1,0:T(8,128)S(1)} %get-tuple-element.61), channel_id=1, source_target_pairs={{0,192},{64,0},{128,64},{192,128},{1,193},{65,1},{129,65},{193,129... | collective-permute-start | bytes 884744 | tf_op jit(solution)/shard_map/density_parts/ppermute | solution.py:403
  40.3 10.1 %collective-permute-start.9 = (f32[6,48,256]{2,1,0:T(8,128)S(1)}, f32[6,48,256]{2,1,0:T(8,128)S(1)}, u32[]{:S(2)}, u32[]{:S(2)}) collective-permute-start(f32[6,48,256]{2,1,0:T(8,128)S(1)} %get-tuple-element.59), channel_id=1, source_target_pairs={{0,64},{64,128},{128,192},{192,0},{1,65},{65,129},{129,193},{193,1... | collective-permute-start | bytes 884744 | tf_op jit(solution)/shard_map/density_parts/ppermute | solution.py:403
  40.6 7.1 %copy-start.1 = (f32[12,192,256]{2,1,0:T(8,128)S(1)}, f32[12,192,256]{2,1,0:T(8,128)}, u32[]{:S(2)}) copy-start(f32[12,192,256]{2,1,0:T(8,128)} %get-tuple-element.38.r) | copy-start | bytes 7077892
  40.6 7.1 %copy-start.3 = (f32[12,192,256]{2,1,0:T(8,128)S(1)}, f32[12,192,256]{2,1,0:T(8,128)}, u32[]{:S(2)}) copy-start(f32[12,192,256]{2,1,0:T(8,128)} %get-tuple-element.48.t_kept) | copy-start | bytes 7077892
  50.4 2.3 %copy-start.8 = (f32[6,48,256]{2,1,0:T(8,128)}, f32[6,48,256]{2,1,0:T(8,128)S(1)}, u32[]{:S(2)}) copy-start(f32[6,48,256]{2,1,0:T(8,128)S(1)} %collective-permute-done.10.refs_4_.refs_6_) | copy-start | bytes 884740
  52.8 53.3 %collective-permute-start.13 = (f32[12,48,256]{2,1,0:T(8,128)}, f32[12,48,256]{2,1,0:T(8,128)S(1)}, u32[]{:S(2)}, u32[]{:S(2)}) collective-permute-start(f32[12,48,256]{2,1,0:T(8,128)} %get-tuple-element.67), channel_id=1, source_target_pairs={{0,64},{64,128},{128,192},{192,0},{1,65},{65,129},{129,193},{193,1... | collective-permute-start | bytes 1769480 | tf_op jit(solution)/shard_map/density_parts/ppermute | solution.py:403
  54.9 51.2 %collective-permute-start.14 = (f32[12,48,256]{2,1,0:T(8,128)}, f32[12,48,256]{2,1,0:T(8,128)S(1)}, u32[]{:S(2)}, u32[]{:S(2)}) collective-permute-start(f32[12,48,256]{2,1,0:T(8,128)} %get-tuple-element.68), channel_id=1, source_target_pairs={{0,128},{64,192},{128,0},{192,64},{1,129},{65,193},{129,1},{193,65... | collective-permute-start | bytes 1769480 | tf_op jit(solution)/shard_map/density_parts/ppermute | solution.py:403
  56.9 49.2 %collective-permute-start.15 = (f32[12,48,256]{2,1,0:T(8,128)}, f32[12,48,256]{2,1,0:T(8,128)S(1)}, u32[]{:S(2)}, u32[]{:S(2)}) collective-permute-start(f32[12,48,256]{2,1,0:T(8,128)} %get-tuple-element.69), channel_id=1, source_target_pairs={{0,192},{64,0},{128,64},{192,128},{1,193},{65,1},{129,65},{193,129... | collective-permute-start | bytes 1769480 | tf_op jit(solution)/shard_map/density_parts/ppermute | solution.py:403
  59.4 8.2 %collective-permute-start.12 = (f32[8,128]{1,0:T(8,128)S(1)}, f32[8,128]{1,0:T(8,128)S(1)}, u32[]{:S(2)}, u32[]{:S(2)}) collective-permute-start(f32[8,128]{1,0:T(8,128)S(1)} %get-tuple-element.62.row), channel_id=1, source_target_pairs={{0,1},{1,0},{2,3},{3,2},{4,5},{5,4},{6,7},{7,6},{8,9},{9,8},{10,11... | collective-permute-start | bytes 12296 | tf_op jit(solution)/shard_map/all_shares/ppermute | solution.py:497
  68.3 27.4 %all-to-all-start = ((f32[32,8,128]{2,1,0:T(8,128)}), f32[32,8,128]{2,1,0:T(8,128)S(1)}, u32[]{:S(2)}, u32[]{:S(2)}) async-start(f32[32,8,128]{2,1,0:T(8,128)} %all_shares.1), calls=%async_computation | async-start | bytes 262144 | tf_op jit(solution)/shard_map/all_shares/all_to_all | solution.py:498
  96.7 9.3 %all-to-all-start.1 = ((f32[4,8,128]{2,1,0:T(8,128)}), f32[4,8,128]{2,1,0:T(8,128)S(1)}, u32[]{:S(2)}, u32[]{:S(2)}) async-start(f32[4,8,128]{2,1,0:T(8,128)} %shard_map.94.coefs), calls=%async_computation.1 | async-start | bytes 32768 | tf_op jit(solution)/shard_map/all_coefficients/all_to_all | solution.py:503
  (5 other events, 7.1 us)
